TPU v7x, 32 devices: a whole 2x2x4 slice. The times are simulated.
32 devices in a mesh: pos: 8 (over z, x), tile: 4 (over y, core).
Axes of the slice: x: 2, y: 2, z: 4, core: 2. Of those that a mesh axis runs over, the one named last changes fastest.
Arguments:
- object_field: float32 [2, 2048, 4096], P(None, 'tile', 'pos'), may hold values from -6 to 6
- probe: float32 [2, 256, 256], replicated, may hold values from -45 to 45
- amplitudes: bfloat16 [4, 8, 32, 256, 256], P('tile', 'pos'), may hold values from 0.099609375 to 3
- corner_rows: int32 [4, 8, 32], P('tile', 'pos'), may hold values from 0 to 511, as said below
- corner_cols: int32 [4, 8, 32], P('tile', 'pos'), may hold values from 0 to 511, as said below
- counts: int32 [4, 8], P('tile', 'pos'), may hold values from 1 to 32, as said below
Outputs:
- object_new: float32 [2, 2048, 4096], P(None, 'tile', 'pos')
- probe_grad: float32 [2, 256, 256], replicated
Inputs may be any that keep to these rules, and one draw needn't show every extreme that they name: Slots from counts[t, p] on are unused. `corner_rows`: counted from the first row of the owner's block. `corner_cols`: counted from the first column of the owner's block.
All inputs are finite; a program needn't handle non-finite values.
Results may differ from a plain program's by a relative error of at most 0.0012.
Values sent between devices are 32-bit elements; how exact they have to be, the bound alone decides.
No kernel may reach another device: no remote copies, remote signals or barrier semaphores. Data moves between devices by JAX's collectives and lax.ppermute only.
A program may use at most 64 MiB of HBM per device.

v0:
```python
import math

import jax
import jax.numpy as jnp
from jax import lax
from jax.sharding import PartitionSpec as P


def passed_along(block, axis, distance):
    devices = range(lax.axis_size(axis))
    route = [(i - distance, i) for i in devices if i - distance in devices]
    return lax.ppermute(block, axis, route)


def dft_tables(points):
    indices = jnp.arange(points, dtype=jnp.int32)
    residues = indices[:, None] * indices[None, :] % points
    angles = residues.astype(jnp.float32) * (2.0 * math.pi / points)
    factor = 1.0 / math.sqrt(points)
    return (
        (jnp.cos(angles) * factor).astype(jnp.bfloat16),
        (-jnp.sin(angles) * factor).astype(jnp.bfloat16),
    )


def left_batch(table_re, table_im, part_re, part_im):

    def product(matrix, operand):
        return jnp.einsum("jk,bkn->bjn", matrix, operand, preferred_element_type=jnp.float32)

    return (
        product(table_re, part_re) - product(table_im, part_im),
        product(table_re, part_im) + product(table_im, part_re),
    )


def right_batch(part_re, part_im, table_re, table_im):

    def product(operand, matrix):
        return jnp.einsum("bmk,kn->bmn", operand, matrix, preferred_element_type=jnp.float32)

    return (
        product(part_re, table_re) - product(part_im, table_im),
        product(part_re, table_im) + product(part_im, table_re),
    )


def shards(object_field, probe, amplitudes, corner_rows, corner_cols, counts):
    patch_size = probe.shape[1]
    rows_here = object_field.shape[1]
    cols_here = object_field.shape[2]
    slot_total = corner_rows.shape[2]
    group_size = 4
    table_re, table_im = dft_tables(patch_size)
    lower_rim = passed_along(object_field[:, :patch_size, :], "tile", -1)
    tall_block = jnp.concatenate([object_field, lower_rim], axis=1)
    right_rim = passed_along(tall_block[:, :, :patch_size], "pos", -1)
    extended = jnp.concatenate([tall_block, right_rim], axis=2)
    slot_rows = corner_rows.reshape(slot_total)
    slot_cols = corner_cols.reshape(slot_total)
    live_count = counts.reshape(())
    amp_slots = amplitudes.reshape(slot_total, patch_size, patch_size)
    probe_re = probe[0]
    probe_im = probe[1]
    zero_index = jnp.zeros((), jnp.int32)

    def read_patch(row_start, col_start):
        return lax.dynamic_slice(
            extended, (zero_index, row_start, col_start), (2, patch_size, patch_size)
        )

    def compute_group(first_slot):
        rows_sel = lax.dynamic_slice_in_dim(slot_rows, first_slot, group_size)
        cols_sel = lax.dynamic_slice_in_dim(slot_cols, first_slot, group_size)
        patches = jax.vmap(read_patch)(rows_sel, cols_sel)
        amp_sel = lax.dynamic_slice_in_dim(amp_slots, first_slot, group_size, 0)
        slot_ids = first_slot + jnp.arange(group_size, dtype=jnp.int32)
        live_mask = (slot_ids < live_count).astype(jnp.float32)[:, None, None]
        patch_re = patches[:, 0]
        patch_im = patches[:, 1]
        exit_re = probe_re * patch_re - probe_im * patch_im
        exit_im = probe_re * patch_im + probe_im * patch_re
        near_re, near_im = left_batch(
            table_re, table_im, exit_re.astype(jnp.bfloat16), exit_im.astype(jnp.bfloat16)
        )
        far_re, far_im = right_batch(
            near_re.astype(jnp.bfloat16), near_im.astype(jnp.bfloat16), table_re, table_im
        )
        modulus = jnp.sqrt(far_re * far_re + far_im * far_im + 0.25)
        ratio = amp_sel.astype(jnp.float32) / modulus
        back_re, back_im = left_batch(
            table_re,
            -table_im,
            (far_re * ratio).astype(jnp.bfloat16),
            (far_im * ratio).astype(jnp.bfloat16),
        )
        new_re, new_im = right_batch(
            back_re.astype(jnp.bfloat16), back_im.astype(jnp.bfloat16), table_re, -table_im
        )
        delta_re = (new_re - exit_re) * live_mask
        delta_im = (new_im - exit_im) * live_mask
        object_re = probe_re * delta_re + probe_im * delta_im
        object_im = probe_re * delta_im - probe_im * delta_re
        probe_part = jnp.stack(
            [
                jnp.sum(patch_re * delta_re + patch_im * delta_im, axis=0),
                jnp.sum(patch_re * delta_im - patch_im * delta_re, axis=0),
            ]
        )
        return (object_re, object_im, probe_part)

    def skip_group(first_slot):
        empty = jnp.zeros((group_size, patch_size, patch_size), jnp.float32)
        return (empty, empty, jnp.zeros((2, patch_size, patch_size), jnp.float32))

    def group_step(group_index, state):
        update_re, update_im, probe_sum = state
        first_slot = (group_index * group_size).astype(jnp.int32)
        object_re, object_im, probe_part = lax.cond(
            first_slot < live_count, compute_group, skip_group, first_slot
        )
        for member in range(group_size):
            row_start = slot_rows[first_slot + member]
            col_start = slot_cols[first_slot + member]
            current_re = lax.dynamic_slice(
                update_re, (row_start, col_start), (patch_size, patch_size)
            )
            update_re = lax.dynamic_update_slice(
                update_re, current_re + object_re[member], (row_start, col_start)
            )
            current_im = lax.dynamic_slice(
                update_im, (row_start, col_start), (patch_size, patch_size)
            )
            update_im = lax.dynamic_update_slice(
                update_im, current_im + object_im[member], (row_start, col_start)
            )
        return (update_re, update_im, probe_sum + probe_part)

    field_shape = (extended.shape[1], extended.shape[2])
    start_state = (
        jnp.zeros(field_shape, jnp.float32),
        jnp.zeros(field_shape, jnp.float32),
        jnp.zeros((2, patch_size, patch_size), jnp.float32),
    )
    update_re, update_im, probe_sum = lax.fori_loop(
        0, slot_total // group_size, group_step, start_state
    )
    update = jnp.stack([update_re, update_im])
    right_back = passed_along(update[:, :, cols_here:], "pos", 1)
    main_part = update[:, :, :cols_here].at[:, :, :patch_size].add(right_back)
    lower_back = passed_along(main_part[:, rows_here:, :], "tile", 1)
    owned_update = main_part[:, :rows_here, :].at[:, :patch_size, :].add(lower_back)
    probe_total = lax.psum(probe_sum, ("pos", "tile"))
    power = jnp.mean(probe_re * probe_re + probe_im * probe_im) + 1e-06
    object_new = object_field + owned_update / power
    probe_grad = probe_total / math.sqrt(lax.axis_size("pos") * lax.axis_size("tile") * slot_total)
    return (object_new, probe_grad)


def solution(mesh):
    return jax.shard_map(
        shards,
        mesh=mesh,
        in_specs=(
            P(None, "tile", "pos"),
            P(),
            P("tile", "pos", None, None, None),
            P("tile", "pos", None),
            P("tile", "pos", None),
            P("tile", "pos"),
        ),
        out_specs=(P(None, "tile", "pos"), P()),
        check_vma=False,
    )
```

profile of v0, /device:TPU:0, one launch (start us, length us, event | category | flops | bytes accessed | tf_op | source)
XLA Modules:
  0.0 908.1 jit_solution(10727796479391937031)
XLA Ops:
  18.9 26.3 %collective-permute-done.1 = f32[2,768,256]{2,1,0:T(8,128)S(1)} collective-permute-done((f32[2,768,256]{2,1,0:T(8,128)}, f32[2,768,256]{2,1,0:T(8,128)S(1)}, u32[]{:S(2)}, u32[]{:S(2)}) %collective-permute-start.1) | collective-permute-done | bytes 1572896 | tf_op jit(solution)/shard_map/ppermute | solution.py:12
  45.1 4.4 pad_maximum_fusion.1
  52.8 578.3 %while.25 = (s32[]{:T(128)}, f32[768,768]{1,0:T(8,128)}, f32[768,768]{1,0:T(8,128)}, f32[2,256,256]{2,1,0:T(8,128)}, s32[32]{0:T(128)S(1)}, /*index=5*/s32[32]{0...) while((s32[]{:T(128)}, f32[768,768]{1,0:T(8,128)}, ...), condition=%wide.region_5.6_spmd.clone.clone, body=%wide.region_0.5_spmd.clone.clone.sunk | while | flops 2163802112 | bytes 69994152 | solution.py:145
  55.4 23.6 %conditional.4 = (f32[4,256,256]{2,1,0:T(8,128)S(1)}, f32[4,256,256]{2,1,0:T(8,128)}, f32[2,256,256]{2,1,0:T(8,128)}) conditional(s32[]{:T(128)} %convert_element_type.187, () %tuple.104, (f32[1,256,256]{2,1,0:T(8,128)}, s32[]{:T(128)}, s32[32]{0:T(128)S(1)}, s32[32]{0:T(128)S(1)}, f32[2,768,768]{2,1,0:T(8,128)}, ...), branch_computations={%region_1.1_spmd, %region_2.4_spmd} | conditional | flops 2160852992 | bytes 53478000 | solution.py:119
  55.7 12.7 %while.24 = (s32[]{:T(128)}, f32[2,768,768]{2,1,0:T(8,128)}, s32[4,3]{1,0:T(4,128)S(1)}, f32[4,2,256,256]{3,2,0,1:T(8,128)S(1)}, s32[]{:T(128)}) while((s32[]{:T(128)}, f32[2,768,768]{2,1,0:T(8,128)}, s32[4,3]{1,0:T(4,128)S(1)}, f32[4,2,256,256]{3,2,0,1:T(8,128)S(1)}, s32[]{:T(128)}) %tuple.108), condition=%wide.while_cond.2, body=%wide.while_body.2.sunk | while | flops 2 | bytes 1048701 | solution.py:68
  119.8 3.9 dynamic_update_slice.109
  130.1 4.0 dynamic_update_slice.111
  138.6 23.6 %conditional.4 = (f32[4,256,256]{2,1,0:T(8,128)S(1)}, f32[4,256,256]{2,1,0:T(8,128)}, f32[2,256,256]{2,1,0:T(8,128)}) conditional(s32[]{:T(128)} %convert_element_type.187, () %tuple.104, (f32[1,256,256]{2,1,0:T(8,128)}, s32[]{:T(128)}, s32[32]{0:T(128)S(1)}, s32[32]{0:T(128)S(1)}, f32[2,768,768]{2,1,0:T(8,128)}, ...), branch_computations={%region_1.1_spmd, %region_2.4_spmd} | conditional | flops 2160852992 | bytes 53478000 | solution.py:119
  138.9 12.7 %while.24 = (s32[]{:T(128)}, f32[2,768,768]{2,1,0:T(8,128)}, s32[4,3]{1,0:T(4,128)S(1)}, f32[4,2,256,256]{3,2,0,1:T(8,128)S(1)}, s32[]{:T(128)}) while((s32[]{:T(128)}, f32[2,768,768]{2,1,0:T(8,128)}, s32[4,3]{1,0:T(4,128)S(1)}, f32[4,2,256,256]{3,2,0,1:T(8,128)S(1)}, s32[]{:T(128)}) %tuple.108), condition=%wide.while_cond.2, body=%wide.while_body.2.sunk | while | flops 2 | bytes 1048701 | solution.py:68
  194.5 3.9 dynamic_update_slice.107
  198.4 3.9 dynamic_update_slice.108
  213.6 3.9 dynamic_update_slice.111
  222.1 23.6 %conditional.4 = (f32[4,256,256]{2,1,0:T(8,128)S(1)}, f32[4,256,256]{2,1,0:T(8,128)}, f32[2,256,256]{2,1,0:T(8,128)}) conditional(s32[]{:T(128)} %convert_element_type.187, () %tuple.104, (f32[1,256,256]{2,1,0:T(8,128)}, s32[]{:T(128)}, s32[32]{0:T(128)S(1)}, s32[32]{0:T(128)S(1)}, f32[2,768,768]{2,1,0:T(8,128)}, ...), branch_computations={%region_1.1_spmd, %region_2.4_spmd} | conditional | flops 2160852992 | bytes 53478000 | solution.py:119
  222.4 12.7 %while.24 = (s32[]{:T(128)}, f32[2,768,768]{2,1,0:T(8,128)}, s32[4,3]{1,0:T(4,128)S(1)}, f32[4,2,256,256]{3,2,0,1:T(8,128)S(1)}, s32[]{:T(128)}) while((s32[]{:T(128)}, f32[2,768,768]{2,1,0:T(8,128)}, s32[4,3]{1,0:T(4,128)S(1)}, f32[4,2,256,256]{3,2,0,1:T(8,128)S(1)}, s32[]{:T(128)}) %tuple.108), condition=%wide.while_cond.2, body=%wide.while_body.2.sunk | while | flops 2 | bytes 1048701 | solution.py:68
  304.8 23.6 %conditional.4 = (f32[4,256,256]{2,1,0:T(8,128)S(1)}, f32[4,256,256]{2,1,0:T(8,128)}, f32[2,256,256]{2,1,0:T(8,128)}) conditional(s32[]{:T(128)} %convert_element_type.187, () %tuple.104, (f32[1,256,256]{2,1,0:T(8,128)}, s32[]{:T(128)}, s32[32]{0:T(128)S(1)}, s32[32]{0:T(128)S(1)}, f32[2,768,768]{2,1,0:T(8,128)}, ...), branch_computations={%region_1.1_spmd, %region_2.4_spmd} | conditional | flops 2160852992 | bytes 53478000 | solution.py:119
  305.1 12.7 %while.24 = (s32[]{:T(128)}, f32[2,768,768]{2,1,0:T(8,128)}, s32[4,3]{1,0:T(4,128)S(1)}, f32[4,2,256,256]{3,2,0,1:T(8,128)S(1)}, s32[]{:T(128)}) while((s32[]{:T(128)}, f32[2,768,768]{2,1,0:T(8,128)}, s32[4,3]{1,0:T(4,128)S(1)}, f32[4,2,256,256]{3,2,0,1:T(8,128)S(1)}, s32[]{:T(128)}) %tuple.108), condition=%wide.while_cond.2, body=%wide.while_body.2.sunk | while | flops 2 | bytes 1048701 | solution.py:68
  374.8 4.0 dynamic_update_slice.110
  380.0 4.0 dynamic_update_slice.111
  405.1 3.9 dynamic_update_slice.105
  431.3 3.9 dynamic_update_slice.109
  558.8 3.9 dynamic_update_slice.110
  634.8 18.8 %collective-permute-done.2 = f32[2,768,256]{2,1,0:T(8,128)S(1)} collective-permute-done((f32[2,768,256]{2,1,0:T(8,128)S(1)}, f32[2,768,256]{2,1,0:T(8,128)S(1)}, u32[]{:S(2)}, u32[]{:S(2)}) %collective-permute-start.2) | collective-permute-done | bytes 1572896 | tf_op jit(solution)/shard_map/ppermute | solution.py:12
  655.6 17.5 %collective-permute-start.3 = (f32[2,256,512]{2,1,0:T(8,128)S(1)}, f32[2,256,512]{2,1,0:T(8,128)S(1)}, u32[]{:S(2)}, u32[]{:S(2)}) collective-permute-start(f32[2,256,512]{2,1,0:T(8,128)S(1)} %slice.208), channel_id=1, source_target_pairs={{0,1},{1,2},{2,3},{4,5},{5,6},{6,7},{8,9},{9,10},{10,11},{12,13},{... | collective-permute-start | bytes 3145736 | tf_op jit(solution)/shard_map/ppermute | solution.py:12
  673.7 220.2 %all-reduce.2.cloned.1.call-done = f32[2,256,256]{2,1,0:T(8,128)} async-done(((f32[2,256,256]{2,1,0:T(8,128)}), f32[2,256,256]{2,1,0:T(8,128)}) %all-reduce.2.cloned.1.call-update) | async-done | bytes 524304 | tf_op jit(solution)/shard_map/psum | solution.py:153
  (399 shorter events, 451.0 us)
Async XLA Ops:
  7.2 2.8 copy-start.8
  7.2 886.7 %all-reduce.2.cloned.1.call-start = ((), (), s32[]{:S(2)}) async-start(), calls=%async_computation | async-start | bytes 1048576 | tf_op jit(solution)/shard_map/psum | solution.py:153
  8.7 4.6 collective-permute-start
  10.2 7.4 copy-start.10
  16.2 28.9 %collective-permute-start.1 = (f32[2,768,256]{2,1,0:T(8,128)}, f32[2,768,256]{2,1,0:T(8,128)S(1)}, u32[]{:S(2)}, u32[]{:S(2)}) collective-permute-start(f32[2,768,256]{2,1,0:T(8,128)} %slice.201), channel_id=1, source_target_pairs={{4,0},{8,4},{12,8},{16,12},{20,16},{24,20},{28,24},{5,1},{9,5},{13... | collective-permute-start | bytes 4718600 | tf_op jit(solution)/shard_map/ppermute | solution.py:12
  49.6 3.2 copy-start.11
  49.6 3.2 copy-start.12
  55.7 12.7 %copy-start.2 = (f32[1,256,256]{2,1,0:T(8,128)S(1)}, f32[1,256,256]{2,1,0:T(8,128)}, u32[]{:S(2)}) copy-start(f32[1,256,256]{2,1,0:T(8,128)} %get-tuple-element.381) | copy-start | bytes 786436 | tf_op jit(solution)/shard_map/while/body/eval_jaxpr/cond
  115.0 19.0 %copy-start.4 = (f32[2,256,256]{2,1,0:T(8,128)S(1)}, f32[2,256,256]{2,1,0:T(8,128)}, u32[]{:S(2)}) copy-start(f32[2,256,256]{2,1,0:T(8,128)} %get-tuple-element.771) | copy-start | bytes 1572868 | tf_op jit(solution)/shard_map/while
  138.9 12.7 %copy-start.2 = (f32[1,256,256]{2,1,0:T(8,128)S(1)}, f32[1,256,256]{2,1,0:T(8,128)}, u32[]{:S(2)}) copy-start(f32[1,256,256]{2,1,0:T(8,128)} %get-tuple-element.381) | copy-start | bytes 786436 | tf_op jit(solution)/shard_map/while/body/eval_jaxpr/cond
  198.4 19.1 %copy-start.4 = (f32[2,256,256]{2,1,0:T(8,128)S(1)}, f32[2,256,256]{2,1,0:T(8,128)}, u32[]{:S(2)}) copy-start(f32[2,256,256]{2,1,0:T(8,128)} %get-tuple-element.771) | copy-start | bytes 1572868 | tf_op jit(solution)/shard_map/while
  222.4 12.7 %copy-start.2 = (f32[1,256,256]{2,1,0:T(8,128)S(1)}, f32[1,256,256]{2,1,0:T(8,128)}, u32[]{:S(2)}) copy-start(f32[1,256,256]{2,1,0:T(8,128)} %get-tuple-element.381) | copy-start | bytes 786436 | tf_op jit(solution)/shard_map/while/body/eval_jaxpr/cond
  281.5 18.7 %copy-start.4 = (f32[2,256,256]{2,1,0:T(8,128)S(1)}, f32[2,256,256]{2,1,0:T(8,128)}, u32[]{:S(2)}) copy-start(f32[2,256,256]{2,1,0:T(8,128)} %get-tuple-element.771) | copy-start | bytes 1572868 | tf_op jit(solution)/shard_map/while
  305.1 12.7 %copy-start.2 = (f32[1,256,256]{2,1,0:T(8,128)S(1)}, f32[1,256,256]{2,1,0:T(8,128)}, u32[]{:S(2)}) copy-start(f32[1,256,256]{2,1,0:T(8,128)} %get-tuple-element.381) | copy-start | bytes 786436 | tf_op jit(solution)/shard_map/while/body/eval_jaxpr/cond
  364.6 19.4 %copy-start.4 = (f32[2,256,256]{2,1,0:T(8,128)S(1)}, f32[2,256,256]{2,1,0:T(8,128)}, u32[]{:S(2)}) copy-start(f32[2,256,256]{2,1,0:T(8,128)} %get-tuple-element.771) | copy-start | bytes 1572868 | tf_op jit(solution)/shard_map/while
  426.5 18.9 %copy-start.4 = (f32[2,256,256]{2,1,0:T(8,128)S(1)}, f32[2,256,256]{2,1,0:T(8,128)}, u32[]{:S(2)}) copy-start(f32[2,256,256]{2,1,0:T(8,128)} %get-tuple-element.771) | copy-start | bytes 1572868 | tf_op jit(solution)/shard_map/while
  487.5 18.5 %copy-start.4 = (f32[2,256,256]{2,1,0:T(8,128)S(1)}, f32[2,256,256]{2,1,0:T(8,128)}, u32[]{:S(2)}) copy-start(f32[2,256,256]{2,1,0:T(8,128)} %get-tuple-element.771) | copy-start | bytes 1572868 | tf_op jit(solution)/shard_map/while
  548.8 19.1 %copy-start.4 = (f32[2,256,256]{2,1,0:T(8,128)S(1)}, f32[2,256,256]{2,1,0:T(8,128)}, u32[]{:S(2)}) copy-start(f32[2,256,256]{2,1,0:T(8,128)} %get-tuple-element.771) | copy-start | bytes 1572868 | tf_op jit(solution)/shard_map/while
  610.3 18.8 %copy-start.4 = (f32[2,256,256]{2,1,0:T(8,128)S(1)}, f32[2,256,256]{2,1,0:T(8,128)}, u32[]{:S(2)}) copy-start(f32[2,256,256]{2,1,0:T(8,128)} %get-tuple-element.771) | copy-start | bytes 1572868 | tf_op jit(solution)/shard_map/while
  631.1 3.2 copy-start
  631.1 3.2 copy-start.1
  632.8 20.8 %collective-permute-start.2 = (f32[2,768,256]{2,1,0:T(8,128)S(1)}, f32[2,768,256]{2,1,0:T(8,128)S(1)}, u32[]{:S(2)}, u32[]{:S(2)}) collective-permute-start(f32[2,768,256]{2,1,0:T(8,128)S(1)} %pad_maximum_fusion.2), channel_id=1, source_target_pairs={{0,4},{4,8},{8,12},{12,16},{16,20},{20,24},{24,28},{1,5},{5,9},{9,... | collective-permute-start | bytes 4718600 | tf_op jit(solution)/shard_map/ppermute | solution.py:12
  655.6 242.0 %collective-permute-start.3 = (f32[2,256,512]{2,1,0:T(8,128)S(1)}, f32[2,256,512]{2,1,0:T(8,128)S(1)}, u32[]{:S(2)}, u32[]{:S(2)}) collective-permute-start(f32[2,256,512]{2,1,0:T(8,128)S(1)} %slice.208), channel_id=1, source_target_pairs={{0,1},{1,2},{2,3},{4,5},{5,6},{6,7},{8,9},{9,10},{10,11},{12,13},{... | collective-permute-start | bytes 3145736 | tf_op jit(solution)/shard_map/ppermute | solution.py:12
  897.6 1.9 copy-start.9
  (14 other events, 13.5 us)
Sparse Core Ops, SparseCore 0:
  673.2 220.6 all-reduce.1
where the time goes:
time: 917 us; the launch traced here: 908 us
  local copies, waits for them, and re-layouts  331 us (36%)
  waiting for transfers between devices  268 us (29%)
  loops' own time  124 us (14%)
  other arithmetic  114 us (12%)
  matrix products  34.4 us (4%)
  starting transfers between devices  21.6 us (2%)
  between operations  14.8 us (2%)
    psum x1, waiting for transfers between devices, shards(): probe_total = lax.psum(probe_sum, ('pos', 'tile'))  220 us
    another operation x1, loops' own time, shards(): lax.fori_loop(0, slot_total // group_size, group_step, start_state)  123 us
    dynamic_update_slice x32, local copies, waits for them, and re-layouts, group_step(): lax.dynamic_update_slice(update_im, current_im + object_im[member], (row_...  122 us
    dynamic_update_slice x32, local copies, waits for them, and re-layouts, group_step(): lax.dynamic_update_slice(update_re, current_re + object_re[member], (row_...  121 us
    gather x48, local copies, waits for them, and re-layouts  50.3 us
    ppermute x4, waiting for transfers between devices, passed_along(): return lax.ppermute(block, axis, route)  48.1 us
    add x32, other arithmetic, group_step(): current_im + object_im[member]  40.5 us
    add x24, other arithmetic, group_step(): current_re + object_re[member]  27.6 us
  transfers between devices with their start and end apart: 5, of which 4 were waited for; matrix products, arithmetic and copies ran while one was open for 1% of the time, Pallas kernels for 0%

commit v1 on v0

v1 whole, which is shorter than its diff:
```python
import functools
import math

import jax
import jax.numpy as jnp
import numpy as np
from jax import lax
from jax.experimental import pallas as pl
from jax.experimental.pallas import tpu as pltpu
from jax.sharding import PartitionSpec as P

LANES = 128
ROWS_STEP = 32


def passed_along(block, axis, distance):
    devices = range(lax.axis_size(axis))
    route = [(i - distance, i) for i in devices if i - distance in devices]
    return lax.ppermute(block, axis, route)


def dft_blocks(points):
    indices = np.arange(points)
    angles = (indices[:, None] * indices[None, :] % points) * (2.0 * math.pi / points)
    factor = 1.0 / math.sqrt(points)
    real = (np.cos(angles) * factor).astype(jnp.bfloat16)
    imag = (-np.sin(angles) * factor).astype(jnp.bfloat16)
    left = np.block([[real, -imag], [imag, real]])
    right = np.block([[real, imag], [-imag, real]])
    return jnp.asarray(left), jnp.asarray(right)


def dot(a, b):
    return jnp.dot(a, b, preferred_element_type=jnp.float32)


def collect(keep, slot_total, order_ref):
    def look(slot, found):
        order_ref[found] = slot
        return found + keep(slot).astype(jnp.int32)

    found = lax.fori_loop(0, slot_total, look, jnp.int32(0))

    order_ref[found] = order_ref[jnp.maximum(found - 1, 0)]
    return found


def run_slots(found, order_ref, rows_ref, cols_ref, probe_ref, amp_ref, left_ref, right_ref,
              field, update, probe_sum, patch, exits, stack, wide):
    size = probe_ref.shape[1]
    blocks = size // LANES

    def read(which, slot):
        row = rows_ref[slot]
        col = cols_ref[slot]
        base = col // LANES
        shift = col % LANES
        for at in range(0, size, ROWS_STEP):
            rows = pl.ds(at, ROWS_STEP)
            lanes = lax.broadcasted_iota(jnp.int32, (ROWS_STEP, LANES), 1)
            own = lanes < LANES - shift
            for block in range(blocks):
                cols = pl.ds(block * LANES, LANES)
                part = []
                for plane in range(2):
                    pair = [
                        pltpu.roll(
                            field[plane, base + k, pl.ds(row + at, ROWS_STEP), :],
                            LANES - shift, 1)
                        for k in (block, block + 1)
                    ]
                    part.append(jnp.where(own, pair[0], pair[1]))
                    patch[which, plane, rows, cols] = part[plane]
                probe_re = probe_ref[0, rows, cols]
                probe_im = probe_ref[1, rows, cols]
                exit_re = probe_re * part[0] - probe_im * part[1]
                exit_im = probe_re * part[1] + probe_im * part[0]
                exits[which, 0, rows, cols] = exit_re
                exits[which, 1, rows, cols] = exit_im
                spot = pl.ds(which * size + block * LANES, LANES)
                stack[rows, spot] = exit_re.astype(jnp.bfloat16)
                stack[pl.ds(size + at, ROWS_STEP), spot] = exit_im.astype(jnp.bfloat16)

    def turn(product):
        for which in range(2):
            for plane in range(2):
                wide[pl.ds(which * size, size), pl.ds(plane * size, size)] = product[
                    plane * size:(plane + 1) * size, which * size:(which + 1) * size
                ].astype(jnp.bfloat16)

    def fix(far, which, slot):
        far_re = far[which * size:(which + 1) * size, :size]
        far_im = far[which * size:(which + 1) * size, size:]
        amp = amp_ref[slot].astype(jnp.float32)
        ratio = amp * lax.rsqrt(far_re * far_re + far_im * far_im + 0.25)
        spot = pl.ds(which * size, size)
        stack[pl.ds(0, size), spot] = (far_re * ratio).astype(jnp.bfloat16)
        stack[pl.ds(size, size), spot] = (far_im * ratio).astype(jnp.bfloat16)

    def add(new, which, slot, weight):
        row = rows_ref[slot]
        col = cols_ref[slot]
        base = col // LANES
        shift = col % LANES
        for at in range(0, size, ROWS_STEP):
            rows = pl.ds(at, ROWS_STEP)
            lanes = lax.broadcasted_iota(jnp.int32, (ROWS_STEP, LANES), 1)
            own = lanes >= shift
            terms = [[], []]
            for block in range(blocks):
                cols = pl.ds(block * LANES, LANES)
                delta = []
                for plane in range(2):
                    start = plane * size + block * LANES
                    value = new[which * size + at:which * size + at + ROWS_STEP, start:start + LANES]
                    value = value - exits[which, plane, rows, cols]
                    delta.append(value if weight is None else value * weight)
                probe_re = probe_ref[0, rows, cols]
                probe_im = probe_ref[1, rows, cols]
                patch_re = patch[which, 0, rows, cols]
                patch_im = patch[which, 1, rows, cols]
                terms[0].append(pltpu.roll(probe_re * delta[0] + probe_im * delta[1], shift, 1))
                terms[1].append(pltpu.roll(probe_re * delta[1] - probe_im * delta[0], shift, 1))
                probe_sum[0, rows, cols] += patch_re * delta[0] + patch_im * delta[1]
                probe_sum[1, rows, cols] += patch_re * delta[1] - patch_im * delta[0]
            for plane in range(2):
                rolled = terms[plane]
                for k in range(blocks + 1):
                    if k == 0:
                        value = jnp.where(own, rolled[0], 0.0)
                    elif k == blocks:
                        value = jnp.where(own, 0.0, rolled[blocks - 1])
                    else:
                        value = jnp.where(own, rolled[k], rolled[k - 1])
                    update[plane, base + k, pl.ds(row + at, ROWS_STEP), :] += value

    def pair_step(step, carry):
        first = order_ref[2 * step]
        second = order_ref[2 * step + 1]
        weight = jnp.where(2 * step + 1 < found, 1.0, 0.0).astype(jnp.float32)
        read(0, first)
        read(1, second)
        turn(dot(left_ref[...], stack[...]))
        far = dot(wide[...], right_ref[...])
        fix(far, 0, first)
        fix(far, 1, second)
        turn(dot(right_ref[...], stack[...]))
        new = dot(wide[...], left_ref[...])
        add(new, 0, first, None)
        add(new, 1, second, weight)
        return carry

    lax.fori_loop(0, (found + 1) // 2, pair_step, 0)


def put(into, row, col, value):
    rows, cols = value.shape[1:]
    for block in range(cols // LANES):
        into[:, col // LANES + block, row:row + rows, :] = value[:, :, block * LANES:(block + 1) * LANES]


def take(out, source, row, col):
    rows, cols = out.shape[1:]
    for block in range(cols // LANES):
        out[:, :, block * LANES:(block + 1) * LANES] = source[:, col // LANES + block, row:row + rows, :]


def near_kernel(rows_ref, cols_ref, count_ref, block_ref, lower_ref, probe_ref, amp_ref, left_ref, right_ref,
                update, probe_sum, order_ref, field, patch, exits, stack, wide):
    size = probe_ref.shape[1]
    rows_here, cols_here = block_ref.shape[1:]
    put(field, 0, 0, block_ref)
    put(field, rows_here, 0, lower_ref)
    update[...] = jnp.zeros_like(update)
    probe_sum[...] = jnp.zeros_like(probe_sum)
    live = count_ref[0]
    found = collect(lambda slot: (slot < live) & (cols_ref[slot] < cols_here - size), rows_ref.shape[0], order_ref)
    run_slots(found, order_ref, rows_ref, cols_ref, probe_ref, amp_ref, left_ref, right_ref,
              field, update, probe_sum, patch, exits, stack, wide)


def rim_kernel(rows_ref, cols_ref, count_ref, block_ref, lower_ref, right_top_ref, right_low_ref, corner_ref,
               probe_ref, amp_ref, left_ref, right_ref, update_in, probe_in,
               own_out, lower_out, right_top_out, right_low_out, corner_out, probe_sum,
               order_ref, field, update, patch, exits, stack, wide):
    size = probe_ref.shape[1]
    rows_here, cols_here = block_ref.shape[1:]
    put(field, 0, 0, block_ref)
    put(field, rows_here, 0, lower_ref)
    put(field, 0, cols_here, right_top_ref)
    put(field, size, cols_here, right_low_ref)
    put(field, rows_here, cols_here, corner_ref)
    inner = cols_here // LANES
    update[:, :inner] = update_in[...]
    update[:, inner:] = jnp.zeros((2, size // LANES) + update.shape[2:], jnp.float32)
    probe_sum[...] = probe_in[...]
    live = count_ref[0]
    found = collect(lambda slot: (slot < live) & (cols_ref[slot] >= cols_here - size), rows_ref.shape[0], order_ref)
    run_slots(found, order_ref, rows_ref, cols_ref, probe_ref, amp_ref, left_ref, right_ref,
              field, update, probe_sum, patch, exits, stack, wide)
    take(own_out, update, 0, 0)
    take(lower_out, update, rows_here, 0)
    take(right_top_out, update, 0, cols_here)
    take(right_low_out, update, size, cols_here)
    take(corner_out, update, rows_here, cols_here)


def finish_kernel(block_ref, own_ref, lower_ref, right_top_ref, right_low_ref, probe_ref, out_ref):
    size = probe_ref.shape[1]
    probe_re = probe_ref[0]
    probe_im = probe_ref[1]
    power = jnp.mean(probe_re * probe_re + probe_im * probe_im) + 1e-06
    scale = 1.0 / power
    for plane in range(2):
        top = own_ref[plane, :size, :] + lower_ref[plane]
        low = own_ref[plane, size:, :]
        out_ref[plane, :size, size:] = block_ref[plane, :size, size:] + top[:, size:] * scale
        out_ref[plane, :size, :size] = block_ref[plane, :size, :size] + (top[:, :size] + right_top_ref[plane]) * scale
        out_ref[plane, size:, size:] = block_ref[plane, size:, size:] + low[:, size:] * scale
        out_ref[plane, size:, :size] = block_ref[plane, size:, :size] + (low[:, :size] + right_low_ref[plane]) * scale


def summed_everywhere(value):
    steps = []
    for axis in ("tile", "pos"):
        size = lax.axis_size(axis)
        masks = []
        mask = 1
        while mask < size:
            masks.append((axis, mask))
            mask *= 2
        steps += masks if axis == "tile" else masks[::-1]

    def partner(block, axis, mask):
        return lax.ppermute(block, axis, [(i, i ^ mask) for i in range(lax.axis_size(axis))])

    def is_low(axis, mask):
        return lax.axis_index(axis) // mask % 2 == 0

    halved = steps[:-2]
    for axis, mask in halved:
        half = value.shape[0] // 2
        low = is_low(axis, mask)
        kept = jnp.where(low, value[:half], value[half:])
        given = jnp.where(low, value[half:], value[:half])
        value = kept + partner(given, axis, mask)
    for axis, mask in steps[-2:]:
        value = value + partner(value, axis, mask)
    for axis, mask in halved[::-1]:
        other = partner(value, axis, mask)
        low = is_low(axis, mask)
        value = jnp.where(low, jnp.concatenate([value, other]), jnp.concatenate([other, value]))
    return value


def shards(object_field, probe, amplitudes, corner_rows, corner_cols, counts):
    size = probe.shape[1]
    rows_here = object_field.shape[1]
    cols_here = object_field.shape[2]
    slots = corner_rows.shape[2]
    left, right = dft_blocks(size)
    slot_rows = corner_rows.reshape(slots)
    slot_cols = corner_cols.reshape(slots)
    live_count = counts.reshape(1)
    amps = amplitudes.reshape(slots, size, size)

    right_top = passed_along(object_field[:, :size, :size], "pos", -1)
    lower = passed_along(object_field[:, :size, :], "tile", -1)
    right_low = passed_along(object_field[:, size:, :size], "pos", -1)
    corner = passed_along(right_top, "tile", -1)

    def spec(n, smem):
        return [pl.BlockSpec(memory_space=pltpu.SMEM)] * smem + [pl.BlockSpec(memory_space=pltpu.VMEM)] * (n - smem)

    def f32(*shape):
        return jax.ShapeDtypeStruct(shape, jnp.float32)

    def work(cols):
        return [
            pltpu.SMEM((slots + 1,), jnp.int32),
            pltpu.VMEM((2, cols // LANES, rows_here + size, LANES), jnp.float32),
        ], [
            pltpu.VMEM((2, 2, size, size), jnp.float32),
            pltpu.VMEM((2, 2, size, size), jnp.float32),
            pltpu.VMEM((2 * size, 2 * size), jnp.bfloat16),
            pltpu.VMEM((2 * size, 2 * size), jnp.bfloat16),
        ]

    def cost(parts):
        return pl.CostEstimate(
            flops=slots // parts * 32 * size**3, bytes_accessed=8 * size * size * slots, transcendentals=0)

    params = pltpu.CompilerParams(vmem_limit_bytes=40 * 1024 * 1024)
    before, after = work(cols_here)
    update, probe_sum = pl.pallas_call(
        near_kernel,
        out_shape=(f32(2, cols_here // LANES, rows_here + size, LANES), f32(2, size, size)),
        in_specs=spec(9, 3),
        out_specs=(pl.BlockSpec(memory_space=pltpu.VMEM),) * 2,
        scratch_shapes=before + after,
        compiler_params=params,
        cost_estimate=cost(2),
        name="near_slots",
    )(slot_rows, slot_cols, live_count, object_field, lower, probe, amps, left, right)

    before, after = work(cols_here + size)
    own, low_part, top_part, side_part, corner_part, probe_sum = pl.pallas_call(
        rim_kernel,
        out_shape=(
            f32(2, rows_here, cols_here), f32(2, size, cols_here), f32(2, size, size),
            f32(2, rows_here - size, size), f32(2, size, size), f32(2, size, size)),
        in_specs=spec(14, 3),
        out_specs=(pl.BlockSpec(memory_space=pltpu.VMEM),) * 6,
        scratch_shapes=before + before[1:] + after,
        compiler_params=params,
        cost_estimate=cost(2),
        name="rim_slots",
    )(slot_rows, slot_cols, live_count, object_field, lower, right_top, right_low, corner,
      probe, amps, left, right, update, probe_sum)

    corner_back = passed_along(corner_part, "tile", 1)
    side_back = passed_along(side_part, "pos", 1)
    low_back = passed_along(low_part, "tile", 1)
    top_back = passed_along(top_part + corner_back, "pos", 1)

    total = summed_everywhere(probe_sum.reshape(2 * size, size)).reshape(2, size, size)
    probe_grad = total / math.sqrt(lax.axis_size("pos") * lax.axis_size("tile") * slots)

    object_new = pl.pallas_call(
        finish_kernel,
        out_shape=f32(2, rows_here, cols_here),
        in_specs=spec(6, 0),
        out_specs=pl.BlockSpec(memory_space=pltpu.VMEM),
        compiler_params=params,
        name="finish",
    )(object_field, own, low_back, top_back, side_back, probe)
    return (object_new, probe_grad)


def solution(mesh):
    return jax.shard_map(
        shards,
        mesh=mesh,
        in_specs=(
            P(None, "tile", "pos"),
            P(),
            P("tile", "pos", None, None, None),
            P("tile", "pos", None),
            P("tile", "pos", None),
            P("tile", "pos"),
        ),
        out_specs=(P(None, "tile", "pos"), P()),
        check_vma=False,
    )
```

time: 917 us -> 146 us (0.16)
  local copies, waits for them, and re-layouts: 331 us -> 15.1 us
  waiting for transfers between devices: 268 us -> 46.9 us
  loops' own time: 124 us -> 0 us
  other arithmetic: 114 us -> 2.72 us
  matrix products: 34.4 us -> 0 us
  Pallas kernels: 0 us -> 32.2 us
  starting transfers between devices: 21.6 us -> 46.3 us
  between operations: 14.8 us -> 1.61 us
    dynamic_update_slice x64 -> x0, local copies, waits for them, and re-layouts: 243 us -> none  [the longest x32 122 us: group_step(): lax.dynamic_update_slice(update_im, current_im + object_im[member], (row_...]
    psum x1 -> x0, waiting for transfers between devices: 220 us -> none  [shards(): probe_total = lax.psum(probe_sum, ('pos', 'tile'))]
    another operation x13 -> x0, loops' own time: 124 us -> none  [the longest x1 123 us: shards(): lax.fori_loop(0, slot_total // group_size, group_step, start_state)]
    add x65 -> x6, other arithmetic: 79.5 us -> 1.13 us  [the longest x3 1.04 us: summed_everywhere(): value = kept + partner(given, axis, mask)]
    gather x48 -> x0, local copies, waits for them, and re-layouts: 50.3 us -> none
    dot_general x64 -> x0, matrix products: 34.4 us -> none  [the longest x32 23.2 us: product(): jnp.einsum('bmk,kn->bmn', operand, matrix, preferred_element_type=jnp.flo...]
    pallas_call x0 -> x3, Pallas kernels: none -> 32.2 us  [the longest x1 15.4 us: shards(): pl.pallas_call(rim_kernel, out_shape=(f32(2, rows_here, cols_here), f32(2...]
    ppermute x0 -> x8, starting transfers between devices: none -> 29.6 us  [partner(): lax.ppermute(block, axis, [(i, i ^ mask) for i in range(lax.axis_size(axi...]
  transfers between devices with their start and end apart: 5 -> 16, of which waited for: 4 -> 10; matrix products, arithmetic and copies ran while one was open for 1% -> 1% of each run, Pallas kernels for 0% -> 10%
where the time goes in v1:
time: 146 us; the launch traced here: 145 us
  waiting for transfers between devices  46.9 us (32%)
  starting transfers between devices  46.3 us (32%)
  Pallas kernels  32.2 us (22%)
  local copies, waits for them, and re-layouts  15.1 us (10%)
  other arithmetic  2.72 us (2%)
  between operations  1.61 us (1%)
    ppermute x8, starting transfers between devices, partner(): lax.ppermute(block, axis, [(i, i ^ mask) for i in range(lax.axis_size(axi...  29.6 us
    ppermute x8, waiting for transfers between devices, passed_along(): return lax.ppermute(block, axis, route)  27.5 us
    ppermute x8, waiting for transfers between devices, partner(): lax.ppermute(block, axis, [(i, i ^ mask) for i in range(lax.axis_size(axi...  19.4 us
    ppermute x8, starting transfers between devices, passed_along(): return lax.ppermute(block, axis, route)  16.7 us
    pallas_call x1, Pallas kernels, shards(): pl.pallas_call(rim_kernel, out_shape=(f32(2, rows_here, cols_here), f32(2...  15.4 us
    pallas_call x1, Pallas kernels, shards(): pl.pallas_call(near_kernel, out_shape=(f32(2, cols_here // LANES, rows_he...  14.8 us
    unnamed x36, local copies, waits for them, and re-layouts  11.6 us
  transfers between devices with their start and end apart: 16, of which 10 were waited for; matrix products, arithmetic and copies ran while one was open for 1% of the time, Pallas kernels for 10%

profile of v1, /device:TPU:0, one launch (start us, length us, event | category | flops | bytes accessed | tf_op | source)
XLA Modules:
  0.0 144.9 jit_solution(4751390858094219716)
XLA Ops:
  0.7 2.4 %slice.35 = f32[2,256,512]{2,1,0:T(8,128)} slice(f32[2,512,512]{2,1,0:T(8,128)} %block_ref.5), slice={[0:2], [0:256], [0:512]} | slice | bytes 2097152 | tf_op jit(solution)/shard_map/slice | solution.py:268
  8.7 14.2 %collective-permute-done.1.right_top_ref = f32[2,256,256]{2,1,0:T(8,128)S(1)} collective-permute-done((f32[2,256,256]{2,1,0:T(8,128)}, f32[2,256,256]{2,1,0:T(8,128)S(1)}, u32[]{:S(2)}, u32[]{:S(2)}) %collective-permute-start.1) | collective-permute-done | bytes 524320 | tf_op jit(solution)/shard_map/ppermute | solution.py:19
  24.3 2.2 %copy-done.6 = bf16[1,1,32,256,256]{4,3,2,1,0:T(8,128)(2,1)S(1)} copy-done((bf16[1,1,32,256,256]{4,3,2,1,0:T(8,128)(2,1)S(1)}, bf16[1,1,32,256,256]{4,3,2,1,0:T(8,128)(2,1)}, u32[]{:S(2)}) %copy-start.6) | copy-done | bytes 4194328
  28.5 14.8 %near_slots.1 = (f32[2,4,768,128]{3,2,1,0:T(8,128)S(1)}, f32[2,256,256]{2,1,0:T(8,128)S(1)}) custom-call(s32[32]{0:T(128)S(1)} %bitcast.13, s32[32]{0:T(128)S(1)} %bitcast.15, s32[1]{0:T(128)} %bitcast.9.count_ref, f32[2,512,512]{2,1,0:T(8,128)S(1)} %copy-done, f32[2,256,512]{2,1,0:T(8,128)} %collective-permute-done.lower_ref, f32[2,256,256]{2,1,0:T(8,128)S(1)} %copy-done.3, ...), custom_call_target="tpu_custom_call" | custom-call | flops 8589934592 | bytes 16777216 | tf_op jit(solution)/shard_map/near_slots/pallas_call | solution.py:295
  43.4 1.6 %copy-done.17 = f32[2,4,768,128]{3,2,1,0:T(8,128)} copy-done((f32[2,4,768,128]{3,2,1,0:T(8,128)}, f32[2,4,768,128]{3,2,1,0:T(8,128)S(1)}, u32[]{:S(2)}) %copy-start.17) | copy-done | bytes 3145752
  46.1 15.4 %rim_slots.1 = (f32[2,512,512]{2,1,0:T(8,128)S(1)}, f32[2,256,512]{2,1,0:T(8,128)S(1)}, f32[2,256,256]{2,1,0:T(8,128)S(1)}, f32[2,256,256]{2,1,0:T(8,128)S(1)}, ...) custom-call(s32[32]{0:T(128)S(1)} %bitcast.14, s32[32]{0:T(128)S(1)} %bitcast.16, s32[1]{0:T(128)} %bitcast.10.count_ref, ...), custom_call_target="tpu_custom_call" | custom-call | flops 8589934592 | bytes 16777216 | tf_op jit(solution)/shard_map/rim_slots/pallas_call | solution.py:307
  61.5 1.3 copy-done.1
  66.2 22.2 %collective-permute-start.8 = (f32[256,256]{1,0:T(8,128)S(1)}, f32[256,256]{1,0:T(8,128)}, u32[]{:S(2)}, u32[]{:S(2)}) collective-permute-start(f32[256,256]{1,0:T(8,128)S(1)} %select_bitcast_fusion), channel_id=1, source_target_pairs={{0,1},{1,0},{2,3},{3,2},{4,5},{5,4},{6,7},{7,6},{8,9},{9,8},{10,11... | collective-permute-start | bytes 786440 | tf_op jit(solution)/shard_map/ppermute | solution.py:235
  88.4 1.3 collective-permute-done.8
  91.4 6.0 %collective-permute-done.9 = f32[128,256]{1,0:T(8,128)S(1)} collective-permute-done((f32[128,256]{1,0:T(8,128)}, f32[128,256]{1,0:T(8,128)S(1)}, u32[]{:S(2)}, u32[]{:S(2)}) %collective-permute-start.9) | collective-permute-done | bytes 131104 | tf_op jit(solution)/shard_map/ppermute | solution.py:235
  97.5 2.0 %collective-permute-start.10 = (f32[64,256]{1,0:T(8,128)S(1)}, f32[64,256]{1,0:T(8,128)S(1)}, u32[]{:S(2)}, u32[]{:S(2)}) collective-permute-start(f32[64,256]{1,0:T(8,128)S(1)} %slice_select_fusion.1), channel_id=1, source_target_pairs={{0,16},{4,20},{8,24},{12,28},{16,0},{20,4},{24,8},{28,12},{1,17},{... | collective-permute-start | bytes 196616 | tf_op jit(solution)/shard_map/ppermute | solution.py:235
  99.5 1.3 collective-permute-start.4
  100.8 2.9 %collective-permute-start.5 = (f32[2,256,256]{2,1,0:T(8,128)}, f32[2,256,256]{2,1,0:T(8,128)S(1)}, u32[]{:S(2)}, u32[]{:S(2)}) collective-permute-start(f32[2,256,256]{2,1,0:T(8,128)} %copy-done.9), channel_id=1, source_target_pairs={{0,1},{1,2},{2,3},{4,5},{5,6},{6,7},{8,9},{9,10},{10,11},{12,13},{... | collective-permute-start | bytes 1572872 | tf_op jit(solution)/shard_map/ppermute | solution.py:19
  104.1 3.7 %collective-permute-start.11 = (f32[64,256]{1,0:T(8,128)S(1)}, f32[64,256]{1,0:T(8,128)S(1)}, u32[]{:S(2)}, u32[]{:S(2)}) collective-permute-start(f32[64,256]{1,0:T(8,128)S(1)} %select_add_fusion.1), channel_id=1, source_target_pairs={{0,8},{4,12},{8,0},{12,4},{16,24},{20,28},{24,16},{28,20},{1,9},{5... | collective-permute-start | bytes 196616 | tf_op jit(solution)/shard_map/ppermute | solution.py:235
  107.8 2.2 %collective-permute-done.11 = f32[64,256]{1,0:T(8,128)S(1)} collective-permute-done((f32[64,256]{1,0:T(8,128)S(1)}, f32[64,256]{1,0:T(8,128)S(1)}, u32[]{:S(2)}, u32[]{:S(2)}) %collective-permute-start.11) | collective-permute-done | bytes 65568 | tf_op jit(solution)/shard_map/ppermute | solution.py:235
  110.1 1.3 collective-permute-start.12
  111.4 3.0 %collective-permute-done.12 = f32[64,256]{1,0:T(8,128)S(1)} collective-permute-done((f32[64,256]{1,0:T(8,128)S(1)}, f32[64,256]{1,0:T(8,128)S(1)}, u32[]{:S(2)}, u32[]{:S(2)}) %collective-permute-start.12) | collective-permute-done | bytes 65568 | tf_op jit(solution)/shard_map/ppermute | solution.py:235
  114.6 5.0 %collective-permute-done.13 = f32[64,256]{1,0:T(8,128)S(1)} collective-permute-done((f32[64,256]{1,0:T(8,128)S(1)}, f32[64,256]{1,0:T(8,128)S(1)}, u32[]{:S(2)}, u32[]{:S(2)}) %collective-permute-start.13) | collective-permute-done | bytes 65568 | tf_op jit(solution)/shard_map/ppermute | solution.py:235
  119.7 3.9 %collective-permute-start.7 = (f32[2,256,256]{2,1,0:T(8,128)}, f32[2,256,256]{2,1,0:T(8,128)S(1)}, u32[]{:S(2)}, u32[]{:S(2)}) collective-permute-start(f32[2,256,256]{2,1,0:T(8,128)} %copy-done.8), channel_id=1, source_target_pairs={{0,4},{4,8},{8,12},{12,16},{16,20},{20,24},{24,28},{1,5},{5,9},{9,... | collective-permute-start | bytes 1572872 | tf_op jit(solution)/shard_map/ppermute | solution.py:19
  123.7 3.4 %collective-permute-start.6 = (f32[2,256,256]{2,1,0:T(8,128)S(1)}, f32[2,256,256]{2,1,0:T(8,128)S(1)}, u32[]{:S(2)}, u32[]{:S(2)}) collective-permute-start(f32[2,256,256]{2,1,0:T(8,128)S(1)} %add.34), channel_id=1, source_target_pairs={{0,4},{4,8},{8,12},{12,16},{16,20},{20,24},{24,28},{1,5},{5,9},{9,... | collective-permute-start | bytes 1572872 | tf_op jit(solution)/shard_map/ppermute | solution.py:19
  127.3 1.5 %collective-permute-done.15 = f32[256,256]{1,0:T(8,128)S(1)} collective-permute-done((f32[256,256]{1,0:T(8,128)S(1)}, f32[256,256]{1,0:T(8,128)S(1)}, u32[]{:S(2)}, u32[]{:S(2)}) %collective-permute-start.15) | collective-permute-done | bytes 262176 | tf_op jit(solution)/shard_map/ppermute | solution.py:235
  129.6 6.6 %collective-permute-done.7.right_low_ref = f32[2,256,256]{2,1,0:T(8,128)S(1)} collective-permute-done((f32[2,256,256]{2,1,0:T(8,128)}, f32[2,256,256]{2,1,0:T(8,128)S(1)}, u32[]{:S(2)}, u32[]{:S(2)}) %collective-permute-start.7) | collective-permute-done | bytes 524320 | tf_op jit(solution)/shard_map/ppermute | solution.py:19
  136.3 6.6 %collective-permute-done.6.right_top_ref = f32[2,256,256]{2,1,0:T(8,128)S(1)} collective-permute-done((f32[2,256,256]{2,1,0:T(8,128)S(1)}, f32[2,256,256]{2,1,0:T(8,128)S(1)}, u32[]{:S(2)}, u32[]{:S(2)}) %collective-permute-start.6) | collective-permute-done | bytes 524320 | tf_op jit(solution)/shard_map/ppermute | solution.py:19
  142.9 1.9 %finish.1 = f32[2,512,512]{2,1,0:T(8,128)} custom-call(f32[2,512,512]{2,1,0:T(8,128)S(1)} %copy-done, f32[2,512,512]{2,1,0:T(8,128)S(1)} %copy-done.2, f32[2,256,512]{2,1,0:T(8,128)S(1)} %collective-permute-done.4.lower_ref, f32[2,256,256]{2,1,0:T(8,128)S(1)} %collective-permute-done.6.right_top_ref, ...), custom_call_target="tpu_custom_call" | custom-call | tf_op jit(solution)/shard_map/finish/pallas_call | solution.py:329
  (61 shorter events, 16.2 us)
Async XLA Ops:
  0.6 3.7 %copy-start = (f32[2,512,512]{2,1,0:T(8,128)S(1)}, f32[2,512,512]{2,1,0:T(8,128)}, u32[]{:S(2)}) copy-start(f32[2,512,512]{2,1,0:T(8,128)} %block_ref.5) | copy-start | bytes 6291460
  0.6 23.6 %copy-start.12 = (s32[1,1,32]{2,1,0:T(1,128)S(1)}, s32[1,1,32]{2,1,0:T(1,128)}, u32[]{:S(2)}) copy-start(s32[1,1,32]{2,1,0:T(1,128)} %param.11) | copy-start | bytes 388
  0.7 23.6 %copy-start.13 = (s32[1,1,32]{2,1,0:T(1,128)S(1)}, s32[1,1,32]{2,1,0:T(1,128)}, u32[]{:S(2)}) copy-start(s32[1,1,32]{2,1,0:T(1,128)} %param.12) | copy-start | bytes 388
  0.7 23.6 %copy-start.3 = (f32[2,256,256]{2,1,0:T(8,128)S(1)}, f32[2,256,256]{2,1,0:T(8,128)}, u32[]{:S(2)}) copy-start(f32[2,256,256]{2,1,0:T(8,128)} %probe_ref.5) | copy-start | bytes 1572868
  3.1 21.1 %collective-permute-start = (f32[2,256,512]{2,1,0:T(8,128)}, f32[2,256,512]{2,1,0:T(8,128)}, u32[]{:S(2)}, u32[]{:S(2)}) collective-permute-start(f32[2,256,512]{2,1,0:T(8,128)} %slice.35), channel_id=1, source_target_pairs={{1,0},{2,1},{3,2},{5,4},{6,5},{7,6},{9,8},{10,9},{11,10},{13,12},{... | collective-permute-start | bytes 3145736 | tf_op jit(solution)/shard_map/ppermute | solution.py:19
  5.5 17.5 %collective-permute-start.1 = (f32[2,256,256]{2,1,0:T(8,128)}, f32[2,256,256]{2,1,0:T(8,128)S(1)}, u32[]{:S(2)}, u32[]{:S(2)}) collective-permute-start(f32[2,256,256]{2,1,0:T(8,128)} %get-tuple-element.19), channel_id=1, source_target_pairs={{4,0},{8,4},{12,8},{16,12},{20,16},{24,20},{28,24},{5,1},{9,5},{13... | collective-permute-start | bytes 1572872 | tf_op jit(solution)/shard_map/ppermute | solution.py:19
  6.7 38.3 %collective-permute-start.2 = (f32[2,256,256]{2,1,0:T(8,128)}, f32[2,256,256]{2,1,0:T(8,128)}, u32[]{:S(2)}, u32[]{:S(2)}) collective-permute-start(f32[2,256,256]{2,1,0:T(8,128)} %get-tuple-element.18), channel_id=1, source_target_pairs={{4,0},{8,4},{12,8},{16,12},{20,16},{24,20},{28,24},{5,1},{9,5},{13... | collective-permute-start | bytes 1572872 | tf_op jit(solution)/shard_map/ppermute | solution.py:19
  22.9 20.4 %copy-start.10 = (f32[2,256,256]{2,1,0:T(8,128)}, f32[2,256,256]{2,1,0:T(8,128)S(1)}, u32[]{:S(2)}) copy-start(f32[2,256,256]{2,1,0:T(8,128)S(1)} %collective-permute-done.1.right_top_ref) | copy-start | bytes 1572868
  22.9 22.1 %collective-permute-start.3 = (f32[2,256,256]{2,1,0:T(8,128)S(1)}, f32[2,256,256]{2,1,0:T(8,128)S(1)}, u32[]{:S(2)}, u32[]{:S(2)}) collective-permute-start(f32[2,256,256]{2,1,0:T(8,128)S(1)} %collective-permute-done.1.right_top_ref), channel_id=1, source_target_pairs={{1,0},{2,1},{3,2},{5,4},{6,5},{7,6},{9,8},{10,9},{11,10},{13,12},{... | collective-permute-start | bytes 1572872 | tf_op jit(solution)/shard_map/ppermute | solution.py:19
  28.5 16.5 %copy-start.15 = (bf16[512,512]{1,0:T(8,128)(2,1)S(1)}, bf16[512,512]{1,0:T(8,128)(2,1)}, u32[]{:S(2)}) copy-start(bf16[512,512]{1,0:T(8,128)(2,1)} %constant.80.clone.left_ref) | copy-start | bytes 1572868
  66.2 23.5 %collective-permute-start.8 = (f32[256,256]{1,0:T(8,128)S(1)}, f32[256,256]{1,0:T(8,128)}, u32[]{:S(2)}, u32[]{:S(2)}) collective-permute-start(f32[256,256]{1,0:T(8,128)S(1)} %select_bitcast_fusion), channel_id=1, source_target_pairs={{0,1},{1,0},{2,3},{3,2},{4,5},{5,4},{6,7},{7,6},{8,9},{9,8},{10,11... | collective-permute-start | bytes 786440 | tf_op jit(solution)/shard_map/ppermute | solution.py:235
  90.7 32.9 %copy-start.5 = (f32[2,256,256]{2,1,0:T(8,128)S(1)}, f32[2,256,256]{2,1,0:T(8,128)}, u32[]{:S(2)}) copy-start(f32[2,256,256]{2,1,0:T(8,128)} %copy-done.4) | copy-start | bytes 1572868
  91.4 6.0 %collective-permute-start.9 = (f32[128,256]{1,0:T(8,128)}, f32[128,256]{1,0:T(8,128)S(1)}, u32[]{:S(2)}, u32[]{:S(2)}) collective-permute-start(f32[128,256]{1,0:T(8,128)} %slice_select_fusion), channel_id=1, source_target_pairs={{0,2},{1,3},{2,0},{3,1},{4,6},{5,7},{6,4},{7,5},{8,10},{9,11},{10,... | collective-permute-start | bytes 393224 | tf_op jit(solution)/shard_map/ppermute | solution.py:235
  97.4 45.5 %copy-start.2 = (f32[2,512,512]{2,1,0:T(8,128)S(1)}, f32[2,512,512]{2,1,0:T(8,128)}, u32[]{:S(2)}) copy-start(f32[2,512,512]{2,1,0:T(8,128)} %copy-done.1) | copy-start | bytes 6291460
  97.5 6.6 %collective-permute-start.10 = (f32[64,256]{1,0:T(8,128)S(1)}, f32[64,256]{1,0:T(8,128)S(1)}, u32[]{:S(2)}, u32[]{:S(2)}) collective-permute-start(f32[64,256]{1,0:T(8,128)S(1)} %slice_select_fusion.1), channel_id=1, source_target_pairs={{0,16},{4,20},{8,24},{12,28},{16,0},{20,4},{24,8},{28,12},{1,17},{... | collective-permute-start | bytes 196616 | tf_op jit(solution)/shard_map/ppermute | solution.py:235
  99.5 36.8 %collective-permute-start.4 = (f32[2,256,512]{2,1,0:T(8,128)}, f32[2,256,512]{2,1,0:T(8,128)S(1)}, u32[]{:S(2)}, u32[]{:S(2)}) collective-permute-start(f32[2,256,512]{2,1,0:T(8,128)} %copy-done.7), channel_id=1, source_target_pairs={{0,1},{1,2},{2,3},{4,5},{5,6},{6,7},{8,9},{9,10},{10,11},{12,13},{... | collective-permute-start | bytes 3145736 | tf_op jit(solution)/shard_map/ppermute | solution.py:19
  100.8 22.8 %collective-permute-start.5 = (f32[2,256,256]{2,1,0:T(8,128)}, f32[2,256,256]{2,1,0:T(8,128)S(1)}, u32[]{:S(2)}, u32[]{:S(2)}) collective-permute-start(f32[2,256,256]{2,1,0:T(8,128)} %copy-done.9), channel_id=1, source_target_pairs={{0,1},{1,2},{2,3},{4,5},{5,6},{6,7},{8,9},{9,10},{10,11},{12,13},{... | collective-permute-start | bytes 1572872 | tf_op jit(solution)/shard_map/ppermute | solution.py:19
  104.1 5.9 %collective-permute-start.11 = (f32[64,256]{1,0:T(8,128)S(1)}, f32[64,256]{1,0:T(8,128)S(1)}, u32[]{:S(2)}, u32[]{:S(2)}) collective-permute-start(f32[64,256]{1,0:T(8,128)S(1)} %select_add_fusion.1), channel_id=1, source_target_pairs={{0,8},{4,12},{8,0},{12,4},{16,24},{20,28},{24,16},{28,20},{1,9},{5... | collective-permute-start | bytes 196616 | tf_op jit(solution)/shard_map/ppermute | solution.py:235
  110.1 4.3 %collective-permute-start.12 = (f32[64,256]{1,0:T(8,128)S(1)}, f32[64,256]{1,0:T(8,128)S(1)}, u32[]{:S(2)}, u32[]{:S(2)}) collective-permute-start(f32[64,256]{1,0:T(8,128)S(1)} %add.41), channel_id=1, source_target_pairs={{0,4},{4,0},{8,12},{12,8},{16,20},{20,16},{24,28},{28,24},{1,5},{5... | collective-permute-start | bytes 196616 | tf_op jit(solution)/shard_map/ppermute | solution.py:235
  114.4 5.2 %collective-permute-start.13 = (f32[64,256]{1,0:T(8,128)S(1)}, f32[64,256]{1,0:T(8,128)S(1)}, u32[]{:S(2)}, u32[]{:S(2)}) collective-permute-start(f32[64,256]{1,0:T(8,128)S(1)} %add.42), channel_id=1, source_target_pairs={{0,16},{4,20},{8,24},{12,28},{16,0},{20,4},{24,8},{28,12},{1,17},{... | collective-permute-start | bytes 196616 | tf_op jit(solution)/shard_map/ppermute | solution.py:235
  119.6 7.5 %collective-permute-start.14 = (f32[128,256]{1,0:T(8,128)S(1)}, f32[128,256]{1,0:T(8,128)S(1)}, u32[]{:S(2)}, u32[]{:S(2)}) collective-permute-start(f32[128,256]{1,0:T(8,128)S(1)} %maximum_select_fusion.2), channel_id=1, source_target_pairs={{0,2},{1,3},{2,0},{3,1},{4,6},{5,7},{6,4},{7,5},{8,10},{9,11},{10,... | collective-permute-start | bytes 393224 | tf_op jit(solution)/shard_map/ppermute | solution.py:235
  119.7 16.6 %collective-permute-start.7 = (f32[2,256,256]{2,1,0:T(8,128)}, f32[2,256,256]{2,1,0:T(8,128)S(1)}, u32[]{:S(2)}, u32[]{:S(2)}) collective-permute-start(f32[2,256,256]{2,1,0:T(8,128)} %copy-done.8), channel_id=1, source_target_pairs={{0,4},{4,8},{8,12},{12,16},{16,20},{20,24},{24,28},{1,5},{5,9},{9,... | collective-permute-start | bytes 1572872 | tf_op jit(solution)/shard_map/ppermute | solution.py:19
  123.7 19.2 %collective-permute-start.6 = (f32[2,256,256]{2,1,0:T(8,128)S(1)}, f32[2,256,256]{2,1,0:T(8,128)S(1)}, u32[]{:S(2)}, u32[]{:S(2)}) collective-permute-start(f32[2,256,256]{2,1,0:T(8,128)S(1)} %add.34), channel_id=1, source_target_pairs={{0,4},{4,8},{8,12},{12,16},{16,20},{20,24},{24,28},{1,5},{5,9},{9,... | collective-permute-start | bytes 1572872 | tf_op jit(solution)/shard_map/ppermute | solution.py:19
  127.2 1.6 %collective-permute-start.15 = (f32[256,256]{1,0:T(8,128)S(1)}, f32[256,256]{1,0:T(8,128)S(1)}, u32[]{:S(2)}, u32[]{:S(2)}) collective-permute-start(f32[256,256]{1,0:T(8,128)S(1)} %maximum_select_fusion.1), channel_id=1, source_target_pairs={{0,1},{1,0},{2,3},{3,2},{4,5},{5,4},{6,7},{7,6},{8,9},{9,8},{10,11... | collective-permute-start | bytes 786440 | tf_op jit(solution)/shard_map/ppermute | solution.py:235
  (10 other events, 11.6 us)

commit v2 on v0

v2 whole, which is shorter than its diff:
```python
import math

import jax
import jax.numpy as jnp
import numpy as np
from jax import lax
from jax.experimental import pallas as pl
from jax.experimental.pallas import tpu as pltpu
from jax.sharding import PartitionSpec as P

LANES = 128
STEP = 32
GROUP = 2


def passed_along(block, axis, distance):
    devices = range(lax.axis_size(axis))
    route = [(i - distance, i) for i in devices if i - distance in devices]
    return lax.ppermute(block, axis, route)


def dft_blocks(points):
    indices = np.arange(points)
    angles = (indices[:, None] * indices[None, :] % points) * (2.0 * math.pi / points)
    factor = 1.0 / math.sqrt(points)
    table_re, table_im = np.cos(angles) * factor, -np.sin(angles) * factor

    def left(rows, cols, sign):
        re, im = table_re[rows, cols], sign * table_im[rows, cols]
        return np.block([[re, -im], [im, re]])

    def right(rows, cols, sign):
        re, im = table_re[rows, cols], sign * table_im[rows, cols]
        return np.block([[re, im], [-im, re]])

    low, even, odd = slice(0, points // 2), slice(0, None, 2), slice(1, None, 2)
    order = np.concatenate([indices[even], indices[odd]])
    sort = np.zeros((points, points))
    sort[indices, order] = 1.0
    return np.stack([
        left(even, low, 1), left(odd, low, 1), right(low, even, 1), right(low, odd, 1),
        left(low, even, -1), left(low, odd, -1), right(even, low, -1), right(odd, low, -1),
        sort, sort.T,
    ]).astype(jnp.bfloat16)


def dot(a, b):
    return jnp.dot(a, b, preferred_element_type=jnp.float32)


def collect(keep, slot_total, order_ref):
    def look(slot, found):
        order_ref[found] = slot
        return found + keep(slot).astype(jnp.int32)

    found = lax.fori_loop(0, slot_total, look, jnp.int32(0))
    last = order_ref[jnp.maximum(found - 1, 0)]
    for extra in range(GROUP - 1):
        order_ref[found + extra] = last
    return found


def run_slots(found, order_ref, rows_ref, cols_ref, probe_ref, amp_ref, mats,
              field, update, probe_sum, scratch):
    size = probe_ref.shape[1]
    half = size // 2
    bf16 = jnp.bfloat16
    patch, xs, far, gs = scratch

    def place(slot):
        col = cols_ref[slot]
        return rows_ref[slot], col // LANES, col % LANES

    def times(re, im, other_re, other_im):
        return re * other_re - im * other_im, re * other_im + im * other_re

    def read(which, slot):
        row, base, shift = place(slot)
        own = lax.broadcasted_iota(jnp.int32, (STEP, LANES), 1) < LANES - shift
        for at in range(0, half, STEP):
            rounded = [[None, None], [None, None]]
            for low in range(2):
                top = low * half + at
                rows = slice(top, top + STEP)
                part = [[None, None], [None, None]]
                for plane in range(2):
                    rolled = [pltpu.roll(field[plane, base + k, pl.ds(row + top, STEP), :], LANES - shift, 1) for k in range(3)]
                    for block in range(2):
                        part[block][plane] = jnp.where(own, rolled[block], rolled[block + 1])
                        patch[which, plane, rows, block * LANES:(block + 1) * LANES] = part[block][plane]
                for block in range(2):
                    cols = slice(block * LANES, (block + 1) * LANES)
                    re, im = times(probe_ref[0, rows, cols], probe_ref[1, rows, cols], *part[block])
                    rounded[block][low] = (re.astype(bf16), im.astype(bf16))
            for block in range(2):
                cols = slice(which * size + block * LANES, which * size + (block + 1) * LANES)
                for plane in range(2):
                    up, low = rounded[block][0][plane], rounded[block][1][plane]
                    rows = slice(plane * half + at, plane * half + at + STEP)
                    xs[0, rows, cols] = up + low
                    xs[1, rows, cols] = up - low

    def group_step(step, carry):
        slots = [order_ref[GROUP * step + i] for i in range(GROUP)]
        for which in range(GROUP):
            read(which, slots[which])
        near = [dot(mats[parity], xs[parity]).astype(bf16) for parity in range(2)]
        folds = [[], []]
        for which in range(GROUP):
            for parity in range(2):
                left = near[parity][:, which * size:which * size + half]
                right = near[parity][:, which * size + half:(which + 1) * size]
                for sign, both in enumerate((left + right, left - right)):
                    folds[sign].append(jnp.concatenate([both[:half], both[half:]], axis=1))
        for sign in range(2):
            far[sign] = dot(jnp.concatenate(folds[sign], axis=0), mats[2 + sign])
        for which in range(GROUP):
            for at in range(0, size, STEP):
                rows = slice(which * size + at, which * size + at + STEP)
                for block in range(2):
                    re = far[block, rows, :half]
                    im = far[block, rows, half:]
                    amp = amp_ref[slots[which], at:at + STEP, block * LANES:(block + 1) * LANES].astype(jnp.float32)
                    ratio = amp * lax.rsqrt(re * re + im * im + 0.25)
                    down = at % half
                    cols = slice(which * size + block * LANES, which * size + (block + 1) * LANES)
                    gs[at // half, down:down + STEP, cols] = (re * ratio).astype(bf16)
                    gs[at // half, half + down:half + down + STEP, cols] = (im * ratio).astype(bf16)
        even = dot(mats[4], gs[0])
        odd = dot(mats[5], gs[1])
        back = (even + odd).astype(bf16), (even - odd).astype(bf16)
        sums = []
        for parity in range(2):
            parts = []
            for which in range(GROUP):
                cols = slice(which * size + parity * half, which * size + (parity + 1) * half)
                for value in back:
                    parts.append(jnp.concatenate([value[:half, cols], value[half:, cols]], axis=1))
            sums.append(dot(jnp.concatenate(parts, axis=0), mats[6 + parity]))
        places = [place(slot) for slot in slots]
        weights = [None] + [jnp.where(GROUP * step + i < found, 1.0, 0.0).astype(jnp.float32) for i in range(1, GROUP)]
        for at in range(0, size, STEP):
            rows = slice(at, at + STEP)
            terms = [[[], []] for _ in range(GROUP)]
            for block in range(2):
                cols = slice(block * LANES, (block + 1) * LANES)
                probe_re = probe_ref[0, rows, cols]
                probe_im = probe_ref[1, rows, cols]
                total = None
                for which in range(GROUP):
                    patch_re = patch[which, 0, rows, cols]
                    patch_im = patch[which, 1, rows, cols]
                    delta = []
                    for plane, value in enumerate(times(probe_re, probe_im, patch_re, patch_im)):
                        a = sums[0][which * size + at:which * size + at + STEP, plane * half:(plane + 1) * half]
                        b = sums[1][which * size + at:which * size + at + STEP, plane * half:(plane + 1) * half]
                        value = (a + b if block == 0 else a - b) - value
                        delta.append(value if which == 0 else value * weights[which])
                    shift = places[which][2]
                    terms[which][0].append(pltpu.roll(probe_re * delta[0] + probe_im * delta[1], shift, 1))
                    terms[which][1].append(pltpu.roll(probe_re * delta[1] - probe_im * delta[0], shift, 1))
                    own_sum = patch_re * delta[0] + patch_im * delta[1], patch_re * delta[1] - patch_im * delta[0]
                    total = own_sum if total is None else (total[0] + own_sum[0], total[1] + own_sum[1])
                probe_sum[0, rows, cols] += total[0]
                probe_sum[1, rows, cols] += total[1]
            for which in range(GROUP):
                row, base, shift = places[which]
                own = lax.broadcasted_iota(jnp.int32, (STEP, LANES), 1) >= shift
                for plane in range(2):
                    first, second = terms[which][plane]
                    update[plane, base, pl.ds(row + at, STEP), :] += jnp.where(own, first, 0.0)
                    update[plane, base + 1, pl.ds(row + at, STEP), :] += jnp.where(own, second, first)
                    update[plane, base + 2, pl.ds(row + at, STEP), :] += jnp.where(own, 0.0, second)
        return carry

    lax.fori_loop(0, (found + GROUP - 1) // GROUP, group_step, 0)


def put(into, row, col, value):
    rows, cols = value.shape[1:]
    for block in range(cols // LANES):
        into[:, col // LANES + block, row:row + rows, :] = value[:, :, block * LANES:(block + 1) * LANES]


def inner_kernel(rows_ref, cols_ref, count_ref, block_ref, probe_ref, amps_ref, mats,
                 update, probe_sum, amp_ref, order_ref, field, *scratch):
    size = probe_ref.shape[1]
    rows_here, cols_here = block_ref.shape[1:]
    put(field, 0, 0, block_ref)
    update[...] = jnp.zeros_like(update)
    probe_sum[...] = jnp.zeros_like(probe_sum)
    live = count_ref[0]
    total = rows_ref.shape[0]
    batch = math.gcd(4, total)

    def sort_amps(step, carry):
        taken = [amps_ref[step * batch + i] for i in range(batch)]
        taken = [dot(mats[8], value).astype(jnp.bfloat16) for value in taken]
        for i in range(batch):
            amp_ref[step * batch + i] = dot(taken[i], mats[9]).astype(jnp.bfloat16)
        return carry

    lax.fori_loop(0, (live + batch - 1) // batch, sort_amps, 0)

    def keep(slot):
        return (slot < live) & (cols_ref[slot] < cols_here - size) & (rows_ref[slot] <= rows_here - size)

    found = collect(keep, total, order_ref)
    run_slots(found, order_ref, rows_ref, cols_ref, probe_ref, amp_ref, mats, field, update, probe_sum, scratch)


def right_kernel(rows_ref, cols_ref, count_ref, block_ref, lower_ref, top_ref, side_ref, corner_ref,
                 probe_ref, amp_ref, mats, update_in, probe_in,
                 update_out, probe_sum, top_out, side_out, corner_out, order_ref, field, update, *scratch):
    size = probe_ref.shape[1]
    rows_here, cols_here = block_ref.shape[1:]
    edge = cols_here // LANES
    put(field, 0, 0, block_ref)
    put(field, rows_here, 0, lower_ref)
    put(field, 0, cols_here, top_ref)
    put(field, size, cols_here, side_ref)
    put(field, rows_here, cols_here, corner_ref)
    update[:, :edge, :rows_here, :] = update_in[...]
    update[:, :edge, rows_here:, :] = jnp.zeros((2, edge, size, LANES), jnp.float32)
    update[:, edge:, :, :] = jnp.zeros((2, size // LANES, rows_here + size, LANES), jnp.float32)
    probe_sum[...] = probe_in[...]
    live = count_ref[0]
    found = collect(lambda slot: (slot < live) & (cols_ref[slot] >= cols_here - size), rows_ref.shape[0], order_ref)
    run_slots(found, order_ref, rows_ref, cols_ref, probe_ref, amp_ref, mats, field, update, probe_sum, scratch)
    update_out[...] = update[:, :edge, :, :]
    top_out[...] = update[:, edge:, :size, :]
    side_out[...] = update[:, edge:, size:rows_here, :]
    corner_out[...] = update[:, edge:, rows_here:, :]


def lower_kernel(rows_ref, cols_ref, count_ref, block_ref, lower_ref, probe_ref, amp_ref, mats, update_in, probe_in,
                 update, low_out, probe_sum, order_ref, field, *scratch):
    size = probe_ref.shape[1]
    rows_here, cols_here = block_ref.shape[1:]
    put(field, 0, 0, block_ref)
    put(field, rows_here, 0, lower_ref)
    update[...] = update_in[...]
    probe_sum[...] = probe_in[...]
    live = count_ref[0]

    def keep(slot):
        return (slot < live) & (cols_ref[slot] < cols_here - size) & (rows_ref[slot] > rows_here - size)

    found = collect(keep, rows_ref.shape[0], order_ref)
    run_slots(found, order_ref, rows_ref, cols_ref, probe_ref, amp_ref, mats, field, update, probe_sum, scratch)
    low_out[...] = update[:, :, rows_here:, :]


def tie_kernel(value_in, other_in, value_out):
    pass


def tie(value, other):
    anywhere = pl.BlockSpec(memory_space=pl.ANY)
    return pl.pallas_call(
        tie_kernel,
        out_shape=jax.ShapeDtypeStruct(value.shape, value.dtype),
        in_specs=[anywhere] * 2,
        out_specs=anywhere,
        input_output_aliases={0: 0},
        compiler_params=pltpu.CompilerParams(vmem_limit_bytes=1024 * 1024),
        name="tie",
    )(value, other)


def finish_kernel(block_ref, update, low_ref, top_ref, side_ref, probe_ref, out_ref):
    size = probe_ref.shape[1]
    rows_here, cols_here = block_ref.shape[1:]
    probe_re = probe_ref[0]
    probe_im = probe_ref[1]
    scale = 1.0 / (jnp.mean(probe_re * probe_re + probe_im * probe_im) + 1e-06)
    for plane in range(2):
        for block in range(cols_here // LANES):
            cols = slice(block * LANES, (block + 1) * LANES)
            top = update[plane, block, :size, :] + low_ref[plane, block]
            side = update[plane, block, size:rows_here, :]
            if block < size // LANES:
                top = top + top_ref[plane, block]
                side = side + side_ref[plane, block]
            out_ref[plane, :size, cols] = block_ref[plane, :size, cols] + top * scale
            out_ref[plane, size:, cols] = block_ref[plane, size:, cols] + side * scale


def partner(block, axis, mask):
    return lax.ppermute(block, axis, [(i, i ^ mask) for i in range(lax.axis_size(axis))])


def is_low(axis, mask):
    return lax.axis_index(axis) // mask % 2 == 0


def halve(value, axis, mask):
    half = value.shape[0] // 2
    low = is_low(axis, mask)
    kept = jnp.where(low, value[:half], value[half:])
    given = jnp.where(low, value[half:], value[:half])
    return kept + partner(given, axis, mask)


def rejoin(value, axis, mask):
    other = partner(value, axis, mask)
    return jnp.where(is_low(axis, mask), jnp.concatenate([value, other]), jnp.concatenate([other, value]))


def masks_of(axis):
    masks = []
    while 2 ** len(masks) < lax.axis_size(axis):
        masks.append((axis, 2 ** len(masks)))
    return masks


def shards(object_field, probe, amplitudes, corner_rows, corner_cols, counts):
    size = probe.shape[1]
    rows_here = object_field.shape[1]
    cols_here = object_field.shape[2]
    slots = corner_rows.shape[2]
    mats = jnp.asarray(dft_blocks(size))
    slot_rows = corner_rows.reshape(slots)
    slot_cols = corner_cols.reshape(slots)
    live_count = counts.reshape(1)
    amps = amplitudes.reshape(slots, size, size)

    right_top = passed_along(object_field[:, :size, :size], "pos", -1)
    right_side = passed_along(object_field[:, size:, :size], "pos", -1)
    lower = passed_along(object_field[:, :size, :], "tile", -1)
    smem = pl.BlockSpec(memory_space=pltpu.SMEM)
    vmem = pl.BlockSpec(memory_space=pltpu.VMEM)

    def f32(*shape):
        return jax.ShapeDtypeStruct(shape, jnp.float32)

    def scratch(blocks, rows, kept):
        held = pltpu.VMEM((2, blocks, rows, LANES), jnp.float32)
        return [pltpu.SMEM((slots + GROUP,), jnp.int32)] + [held] * kept + [
            pltpu.VMEM((GROUP, 2, size, size), jnp.float32),
            pltpu.VMEM((2, size, GROUP * size), jnp.bfloat16),
            pltpu.VMEM((2, GROUP * size, size), jnp.float32),
            pltpu.VMEM((2, size, GROUP * size), jnp.bfloat16),
        ]

    def call(kernel, name, outs, held, *arrays):
        return pl.pallas_call(
            kernel,
            out_shape=outs,
            in_specs=[smem] * 3 + [vmem] * len(arrays),
            out_specs=[vmem] * len(outs),
            scratch_shapes=scratch(*held),
            compiler_params=params,
            cost_estimate=pl.CostEstimate(
                flops=slots // 4 * 32 * size**3, bytes_accessed=8 * size * size * slots, transcendentals=0),
            name=name,
        )(slot_rows, slot_cols, live_count, *arrays)

    params = pltpu.CompilerParams(vmem_limit_bytes=24 * 1024 * 1024)
    edge = cols_here // LANES
    rim = size // LANES
    plane = f32(2, size, size)

    update, probe_sum, amps = call(
        inner_kernel, "inner_slots", [f32(2, edge, rows_here, LANES), plane, jax.ShapeDtypeStruct(amps.shape, amps.dtype)],
        (edge, rows_here, 1), object_field, probe, amps, mats)

    right_top = tie(right_top, probe_sum)
    corner = passed_along(right_top, "tile", -1)

    update, probe_sum, top_part, side_part, corner_part = call(
        right_kernel, "right_slots",
        [f32(2, edge, rows_here + size, LANES), plane, f32(2, rim, size, LANES),
         f32(2, rim, rows_here - size, LANES), f32(2, rim, size, LANES)],
        (edge + rim, rows_here + size, 2),
        object_field, lower, right_top, right_side, corner, probe, amps, mats, update, probe_sum)

    corner_back = passed_along(corner_part, "tile", 1)
    side_back = passed_along(side_part, "pos", 1)

    update, low_part, probe_sum = call(
        lower_kernel, "lower_slots",
        [f32(2, edge, rows_here + size, LANES), f32(2, edge, size, LANES), plane],
        (edge, rows_here + size, 1), object_field, lower, probe, amps, mats, update, probe_sum)

    low_back = passed_along(low_part, "tile", 1)
    top_back = passed_along(top_part + tie(corner_back, probe_sum), "pos", 1)

    tile_steps = masks_of("tile")
    pos_steps = masks_of("pos")[::-1]

    def sum_all(value):
        for step in tile_steps + pos_steps[:-2]:
            value = halve(value, *step)
        for step in pos_steps[-2:]:
            value = value + partner(value, *step)
        value = value * (1.0 / math.sqrt(lax.axis_size("pos") * lax.axis_size("tile") * slots))
        for step in pos_steps[:-2][::-1] + tile_steps[::-1]:
            value = rejoin(value, *step)
        return value

    probe_grad = lax.cond(live_count[0] >= 1, sum_all, jnp.zeros_like, probe_sum.reshape(2 * size, size))

    object_new = pl.pallas_call(
        finish_kernel,
        out_shape=f32(2, rows_here, cols_here),
        in_specs=[vmem] * 6,
        out_specs=vmem,
        compiler_params=params,
        name="finish",
    )(object_field, update, low_back, top_back, side_back, probe)
    return (object_new, probe_grad.reshape(2, size, size))


def solution(mesh):
    return jax.shard_map(
        shards,
        mesh=mesh,
        in_specs=(
            P(None, "tile", "pos"),
            P(),
            P("tile", "pos", None, None, None),
            P("tile", "pos", None),
            P("tile", "pos", None),
            P("tile", "pos"),
        ),
        out_specs=(P(None, "tile", "pos"), P()),
        check_vma=False,
    )
```

time: 917 us -> 133 us (0.15); the launches traced: 908 us -> 134 us
  local copies, waits for them, and re-layouts: 331 us -> 8.28 us
  waiting for transfers between devices: 268 us -> 36.6 us
  loops' own time: 124 us -> 0.1 us
  other arithmetic: 114 us -> 4.69 us
  starting transfers between devices: 21.6 us -> 65.1 us
  matrix products: 34.4 us -> 0 us
  Pallas kernels: 0 us -> 18.2 us
  between operations: 14.8 us -> 1.46 us
    dynamic_update_slice x64 -> x0, local copies, waits for them, and re-layouts: 243 us -> none  [the longest x32 122 us: group_step(): lax.dynamic_update_slice(update_im, current_im + object_im[member], (row_...]
    psum x1 -> x0, waiting for transfers between devices: 220 us -> none  [shards(): probe_total = lax.psum(probe_sum, ('pos', 'tile'))]
    another operation x13 -> x1, loops' own time: 124 us -> 0.1 us  [shards(): lax.cond(live_count[0] >= 1, sum_all, jnp.zeros_like, probe_sum.reshape(2...]
    add x65 -> x5, other arithmetic: 79.5 us -> 2.06 us  [the longest x3 1.2 us: halve(): return kept + partner(given, axis, mask)]
    gather x48 -> x0, local copies, waits for them, and re-layouts: 50.3 us -> none
    dot_general x64 -> x0, matrix products: 34.4 us -> none  [the longest x32 23.2 us: product(): jnp.einsum('bmk,kn->bmn', operand, matrix, preferred_element_type=jnp.flo...]
    ppermute x4 -> x8, waiting for transfers between devices: 48.1 us -> 13.8 us  [passed_along(): return lax.ppermute(block, axis, route)]
    ppermute x0 -> x8, waiting for transfers between devices: none -> 22.8 us  [partner(): lax.ppermute(block, axis, [(i, i ^ mask) for i in range(lax.axis_size(axi...]
  transfers between devices with their start and end apart: 5 -> 16, of which waited for: 4 -> 10; matrix products, arithmetic and copies ran while one was open for 1% -> 4% of each run, Pallas kernels for 0% -> 8%
where the time goes in v2:
time: 133 us; the launch traced here: 134 us
  starting transfers between devices  65.1 us (49%)
  waiting for transfers between devices  36.6 us (28%)
  Pallas kernels  18.2 us (14%)
  local copies, waits for them, and re-layouts  8.28 us (6%)
  other arithmetic  4.69 us (4%)
  between operations  1.46 us (1%)
    ppermute x8, starting transfers between devices, passed_along(): return lax.ppermute(block, axis, route)  43.6 us
    ppermute x8, waiting for transfers between devices, partner(): lax.ppermute(block, axis, [(i, i ^ mask) for i in range(lax.axis_size(axi...  22.8 us
    ppermute x8, starting transfers between devices, partner(): lax.ppermute(block, axis, [(i, i ^ mask) for i in range(lax.axis_size(axi...  21.5 us
    pallas_call x3, Pallas kernels, call(): pl.pallas_call(kernel, out_shape=outs, in_specs=[smem] * 3 + [vmem] * len...  15 us
    ppermute x8, waiting for transfers between devices, passed_along(): return lax.ppermute(block, axis, route)  13.8 us
    unnamed x18, local copies, waits for them, and re-layouts  6.76 us
    pallas_call x1, Pallas kernels, shards(): pl.pallas_call(finish_kernel, out_shape=f32(2, rows_here, cols_here), in_...  3.16 us
  transfers between devices with their start and end apart: 16, of which 10 were waited for; matrix products, arithmetic and copies ran while one was open for 4% of the time, Pallas kernels for 8%

profile of v2, /device:TPU:0, one launch (start us, length us, event | category | flops | bytes accessed | tf_op | source)
XLA Modules:
  0.0 134.4 jit_solution(6145613354754893441)
XLA Ops:
  7.0 2.2 %copy-done.5 = bf16[1,1,32,256,256]{4,3,2,1,0:T(8,128)(2,1)S(1)} copy-done((bf16[1,1,32,256,256]{4,3,2,1,0:T(8,128)(2,1)S(1)}, bf16[1,1,32,256,256]{4,3,2,1,0:T(8,128)(2,1)}, u32[]{:S(2)}) %copy-start.5) | copy-done | bytes 4194328
  9.1 6.1 %inner_slots.1 = (f32[2,4,512,128]{3,2,1,0:T(8,128)S(1)}, f32[2,256,256]{2,1,0:T(8,128)S(1)}, bf16[32,256,256]{2,1,0:T(8,128)(2,1)S(1)}) custom-call(s32[32]{0:T(128)S(1)} %bitcast.14, s32[32]{0:T(128)S(1)} %bitcast.17, s32[1]{0:T(128)} %bitcast.10.count_ref, f32[2,512,512]{2,1,0:T(8,128)S(1)} %copy-done, f32[2,256,256]{2,1,0:T(8,128)S(1)} %copy-done.3, ...), custom_call_target="tpu_custom_call" | custom-call | flops 4294967296 | bytes 16777216 | tf_op jit(solution)/shard_map/inner_slots/pallas_call | solution.py:347
  15.2 4.6 %collective-permute-done.9.value_in = f32[2,256,256]{2,1,0:T(8,128)S(1)} collective-permute-done((f32[2,256,256]{2,1,0:T(8,128)S(1)}, f32[2,256,256]{2,1,0:T(8,128)S(1)}, u32[]{:S(2)}, u32[]{:S(2)}) %collective-permute-start.9) | collective-permute-done | bytes 524320 | tf_op jit(solution)/shard_map/ppermute | solution.py:19
  21.2 9.1 %collective-permute-done.10.side_ref = f32[2,256,256]{2,1,0:T(8,128)S(1)} collective-permute-done((f32[2,256,256]{2,1,0:T(8,128)S(1)}, f32[2,256,256]{2,1,0:T(8,128)S(1)}, u32[]{:S(2)}, u32[]{:S(2)}) %collective-permute-start.10) | collective-permute-done | bytes 524320 | tf_op jit(solution)/shard_map/ppermute | solution.py:19
  30.3 4.5 %right_slots.1 = (f32[2,4,768,128]{3,2,1,0:T(8,128)S(1)}, f32[2,256,256]{2,1,0:T(8,128)S(1)}, f32[2,2,256,128]{3,2,1,0:T(8,128)S(1)}, f32[2,2,256,128]{3,2,1,0:T(8,128)}, f32[2,2,256,128]{3,2,1,0:T(8,128)S(1)}) custom-call(s32[32]{0:T(128)S(1)} %bitcast.15, s32[32]{0:T(128)S(1)} %bitcast.18, s32[1]{0:T(128)} %bitcast.11.count_ref, ...), custom_call_target="tpu_custom_call" | custom-call | flops 4294967296 | bytes 16777216 | tf_op jit(solution)/shard_map/right_slots/pallas_call | solution.py:347
  34.7 23.3 %collective-permute-start.13 = (f32[2,2,256,128]{3,2,1,0:T(8,128)S(1)}, f32[2,2,256,128]{3,2,1,0:T(8,128)S(1)}, u32[]{:S(2)}, u32[]{:S(2)}) collective-permute-start(f32[2,2,256,128]{3,2,1,0:T(8,128)S(1)} %get-tuple-element.27), channel_id=1, source_target_pairs={{0,1},{1,2},{2,3},{4,5},{5,6},{6,7},{8,9},{9,10},{10,11},{12,13},{... | collective-permute-start | bytes 1572872 | tf_op jit(solution)/shard_map/ppermute | solution.py:19
  58.1 4.5 %lower_slots.1 = (f32[2,4,768,128]{3,2,1,0:T(8,128)S(1)}, f32[2,4,256,128]{3,2,1,0:T(8,128)}, f32[2,256,256]{2,1,0:T(8,128)}) custom-call(s32[32]{0:T(128)S(1)} %bitcast.16, s32[32]{0:T(128)S(1)} %bitcast.19, s32[1]{0:T(128)} %bitcast.12.count_ref, f32[2,512,512]{2,1,0:T(8,128)S(1)} %copy-done, f32[2,256,512]{2,1,0:T(8,128)S(1)} %collective-permute-done.8.lower_ref, ...), custom_call_target="tpu_custom_call" | custom-call | flops 4294967296 | bytes 16777216 | tf_op jit(solution)/shard_map/lower_slots/pallas_call | solution.py:347
  62.5 1.6 %copy-done.1 = f32[2,4,768,128]{3,2,1,0:T(8,128)} copy-done((f32[2,4,768,128]{3,2,1,0:T(8,128)}, f32[2,4,768,128]{3,2,1,0:T(8,128)S(1)}, u32[]{:S(2)}) %copy-start.1) | copy-done | bytes 3145752
  64.2 4.0 %collective-permute-start.12 = (f32[2,4,256,128]{3,2,1,0:T(8,128)}, f32[2,4,256,128]{3,2,1,0:T(8,128)S(1)}, u32[]{:S(2)}, u32[]{:S(2)}) collective-permute-start(f32[2,4,256,128]{3,2,1,0:T(8,128)} %get-tuple-element.25), channel_id=1, source_target_pairs={{0,1},{1,2},{2,3},{4,5},{5,6},{6,7},{8,9},{9,10},{10,11},{12,13},{... | collective-permute-start | bytes 3145736 | tf_op jit(solution)/shard_map/ppermute | solution.py:19
  68.1 8.9 %collective-permute-start.15 = (f32[2,2,256,128]{3,2,1,0:T(8,128)}, f32[2,2,256,128]{3,2,1,0:T(8,128)}, u32[]{:S(2)}, u32[]{:S(2)}) collective-permute-start(f32[2,2,256,128]{3,2,1,0:T(8,128)} %get-tuple-element.29), channel_id=1, source_target_pairs={{0,4},{4,8},{8,12},{12,16},{16,20},{20,24},{24,28},{1,5},{5,9},{9,... | collective-permute-start | bytes 1572872 | tf_op jit(solution)/shard_map/ppermute | solution.py:19
  77.9 2.1 %collective-permute-start.14 = (f32[2,2,256,128]{3,2,1,0:T(8,128)}, f32[2,2,256,128]{3,2,1,0:T(8,128)}, u32[]{:S(2)}, u32[]{:S(2)}) collective-permute-start(f32[2,2,256,128]{3,2,1,0:T(8,128)} %add.34), channel_id=1, source_target_pairs={{0,4},{4,8},{8,12},{12,16},{16,20},{20,24},{24,28},{1,5},{5,9},{9,... | collective-permute-start | bytes 1572872 | tf_op jit(solution)/shard_map/ppermute | solution.py:19
  80.0 48.3 %conditional.1 = (f32[2,256,256]{2,1,0:T(8,128)}) conditional(s32[]{:T(128)} %bitcast.7, () %tuple.16, f32[2,256,256]{2,1,0:T(8,128)} %get-tuple-element.28.other_in), branch_computations={%region_0.0_spmd, %region_1.2_spmd} | conditional | flops 1081408 | bytes 9634763 | solution.py:402
  84.7 5.7 %collective-permute-done.1 = f32[128,256]{1,0:T(8,128)S(1)} collective-permute-done((f32[128,256]{1,0:T(8,128)}, f32[128,256]{1,0:T(8,128)S(1)}, u32[]{:S(2)}, u32[]{:S(2)}) %collective-permute-start.1) | collective-permute-done | bytes 131104 | tf_op jit(solution)/shard_map/cond/branch_1_fun/ppermute | solution.py:290
  90.5 6.6 %collective-permute-start.2 = (f32[64,256]{1,0:T(8,128)S(1)}, f32[64,256]{1,0:T(8,128)S(1)}, u32[]{:S(2)}, u32[]{:S(2)}) collective-permute-start(f32[64,256]{1,0:T(8,128)S(1)} %slice_select_fusion.1), channel_id=1, source_target_pairs={{0,16},{4,20},{8,24},{12,28},{16,0},{20,4},{24,8},{28,12},{1,17},{... | collective-permute-start | bytes 196616 | tf_op jit(solution)/shard_map/cond/branch_1_fun/ppermute | solution.py:290
  97.1 2.2 %collective-permute-done.2 = f32[64,256]{1,0:T(8,128)S(1)} collective-permute-done((f32[64,256]{1,0:T(8,128)S(1)}, f32[64,256]{1,0:T(8,128)S(1)}, u32[]{:S(2)}, u32[]{:S(2)}) %collective-permute-start.2) | collective-permute-done | bytes 65568 | tf_op jit(solution)/shard_map/cond/branch_1_fun/ppermute | solution.py:290
  99.3 4.2 %collective-permute-start.3 = (f32[64,256]{1,0:T(8,128)S(1)}, f32[64,256]{1,0:T(8,128)S(1)}, u32[]{:S(2)}, u32[]{:S(2)}) collective-permute-start(f32[64,256]{1,0:T(8,128)S(1)} %select_add_fusion.1), channel_id=1, source_target_pairs={{0,8},{4,12},{8,0},{12,4},{16,24},{20,28},{24,16},{28,20},{1,9},{5... | collective-permute-start | bytes 196616 | tf_op jit(solution)/shard_map/cond/branch_1_fun/ppermute | solution.py:290
  103.5 2.2 %collective-permute-done.3 = f32[64,256]{1,0:T(8,128)S(1)} collective-permute-done((f32[64,256]{1,0:T(8,128)S(1)}, f32[64,256]{1,0:T(8,128)S(1)}, u32[]{:S(2)}, u32[]{:S(2)}) %collective-permute-start.3) | collective-permute-done | bytes 65568 | tf_op jit(solution)/shard_map/cond/branch_1_fun/ppermute | solution.py:290
  105.7 7.1 %collective-permute-start.4 = (f32[64,256]{1,0:T(8,128)S(1)}, f32[64,256]{1,0:T(8,128)S(1)}, u32[]{:S(2)}, u32[]{:S(2)}) collective-permute-start(f32[64,256]{1,0:T(8,128)S(1)} %add.31), channel_id=1, source_target_pairs={{0,4},{4,0},{8,12},{12,8},{16,20},{20,16},{24,28},{28,24},{1,5},{5... | collective-permute-start | bytes 196616 | tf_op jit(solution)/shard_map/cond/branch_1_fun/ppermute | solution.py:290
  112.8 2.2 %collective-permute-done.4 = f32[64,256]{1,0:T(8,128)S(1)} collective-permute-done((f32[64,256]{1,0:T(8,128)S(1)}, f32[64,256]{1,0:T(8,128)S(1)}, u32[]{:S(2)}, u32[]{:S(2)}) %collective-permute-start.4) | collective-permute-done | bytes 65568 | tf_op jit(solution)/shard_map/cond/branch_1_fun/ppermute | solution.py:290
  115.1 3.4 %collective-permute-start.5 = (f32[64,256]{1,0:T(8,128)S(1)}, f32[64,256]{1,0:T(8,128)S(1)}, u32[]{:S(2)}, u32[]{:S(2)}) collective-permute-start(f32[64,256]{1,0:T(8,128)S(1)} %add_multiply_fusion), channel_id=1, source_target_pairs={{0,16},{4,20},{8,24},{12,28},{16,0},{20,4},{24,8},{28,12},{1,17},{... | collective-permute-start | bytes 196616 | tf_op jit(solution)/shard_map/cond/branch_1_fun/ppermute | solution.py:290
  118.5 2.2 %collective-permute-done.5 = f32[64,256]{1,0:T(8,128)S(1)} collective-permute-done((f32[64,256]{1,0:T(8,128)S(1)}, f32[64,256]{1,0:T(8,128)S(1)}, u32[]{:S(2)}, u32[]{:S(2)}) %collective-permute-start.5) | collective-permute-done | bytes 65568 | tf_op jit(solution)/shard_map/cond/branch_1_fun/ppermute | solution.py:290
  120.9 5.0 %collective-permute-done.6 = f32[128,256]{1,0:T(8,128)S(1)} collective-permute-done((f32[128,256]{1,0:T(8,128)S(1)}, f32[128,256]{1,0:T(8,128)S(1)}, u32[]{:S(2)}, u32[]{:S(2)}) %collective-permute-start.6) | collective-permute-done | bytes 131104 | tf_op jit(solution)/shard_map/cond/branch_1_fun/ppermute | solution.py:290
  128.3 1.9 %copy-done.2 = f32[2,4,768,128]{3,2,1,0:T(8,128)S(1)} copy-done((f32[2,4,768,128]{3,2,1,0:T(8,128)S(1)}, f32[2,4,768,128]{3,2,1,0:T(8,128)}, u32[]{:S(2)}) %copy-start.2) | copy-done | bytes 3145752
  131.3 3.2 %finish.1 = f32[2,512,512]{2,1,0:T(8,128)} custom-call(f32[2,512,512]{2,1,0:T(8,128)S(1)} %copy-done, f32[2,4,768,128]{3,2,1,0:T(8,128)S(1)} %copy-done.2, f32[2,4,256,128]{3,2,1,0:T(8,128)S(1)} %collective-permute-done.12.low_ref, f32[2,2,256,128]{3,2,1,0:T(8,128)} %collective-permute-done.14.top_ref, f32[2,2,256,128]{3,2,1,0:T(8,128)} %collective-permute-done.15.side_ref, ...), custom_call_target="tpu_custom_call" | custom-call | tf_op jit(solution)/shard_map/finish/pallas_call | solution.py:404
  (47 shorter events, 15.9 us)
Async XLA Ops:
  0.6 2.9 %copy-start = (f32[2,512,512]{2,1,0:T(8,128)S(1)}, f32[2,512,512]{2,1,0:T(8,128)}, u32[]{:S(2)}) copy-start(f32[2,512,512]{2,1,0:T(8,128)} %block_ref.7) | copy-start | bytes 6291460
  0.6 6.3 %copy-start.8 = (bf16[10,256,256]{2,1,0:T(8,128)(2,1)S(1)}, bf16[10,256,256]{2,1,0:T(8,128)(2,1)}, u32[]{:S(2)}) copy-start(bf16[10,256,256]{2,1,0:T(8,128)(2,1)} %constant.82.clone.mats) | copy-start | bytes 3932164
  0.7 6.3 %copy-start.6 = (s32[1,1,32]{2,1,0:T(1,128)S(1)}, s32[1,1,32]{2,1,0:T(1,128)}, u32[]{:S(2)}) copy-start(s32[1,1,32]{2,1,0:T(1,128)} %param.12) | copy-start | bytes 388
  0.7 6.3 %copy-start.7 = (s32[1,1,32]{2,1,0:T(1,128)S(1)}, s32[1,1,32]{2,1,0:T(1,128)}, u32[]{:S(2)}) copy-start(s32[1,1,32]{2,1,0:T(1,128)} %param.13) | copy-start | bytes 388
  0.7 6.3 %copy-start.3 = (f32[2,256,256]{2,1,0:T(8,128)S(1)}, f32[2,256,256]{2,1,0:T(8,128)}, u32[]{:S(2)}) copy-start(f32[2,256,256]{2,1,0:T(8,128)} %probe_ref.7) | copy-start | bytes 1572868
  2.1 17.7 %collective-permute-start.9 = (f32[2,256,256]{2,1,0:T(8,128)S(1)}, f32[2,256,256]{2,1,0:T(8,128)S(1)}, u32[]{:S(2)}, u32[]{:S(2)}) collective-permute-start(f32[2,256,256]{2,1,0:T(8,128)S(1)} %get-tuple-element.31), channel_id=1, source_target_pairs={{4,0},{8,4},{12,8},{16,12},{20,16},{24,20},{28,24},{5,1},{9,5},{13... | collective-permute-start | bytes 1572872 | tf_op jit(solution)/shard_map/ppermute | solution.py:19
  3.7 26.6 %collective-permute-start.8 = (f32[2,256,512]{2,1,0:T(8,128)S(1)}, f32[2,256,512]{2,1,0:T(8,128)S(1)}, u32[]{:S(2)}, u32[]{:S(2)}) collective-permute-start(f32[2,256,512]{2,1,0:T(8,128)S(1)} %slice.35), channel_id=1, source_target_pairs={{1,0},{2,1},{3,2},{5,4},{6,5},{7,6},{9,8},{10,9},{11,10},{13,12},{... | collective-permute-start | bytes 3145736 | tf_op jit(solution)/shard_map/ppermute | solution.py:19
  5.0 25.3 %collective-permute-start.10 = (f32[2,256,256]{2,1,0:T(8,128)S(1)}, f32[2,256,256]{2,1,0:T(8,128)S(1)}, u32[]{:S(2)}, u32[]{:S(2)}) collective-permute-start(f32[2,256,256]{2,1,0:T(8,128)S(1)} %get-tuple-element.30), channel_id=1, source_target_pairs={{4,0},{8,4},{12,8},{16,12},{20,16},{24,20},{28,24},{5,1},{9,5},{13... | collective-permute-start | bytes 1572872 | tf_op jit(solution)/shard_map/ppermute | solution.py:19
  6.9 2.2 %copy-start.5 = (bf16[1,1,32,256,256]{4,3,2,1,0:T(8,128)(2,1)S(1)}, bf16[1,1,32,256,256]{4,3,2,1,0:T(8,128)(2,1)}, u32[]{:S(2)}) copy-start(bf16[1,1,32,256,256]{4,3,2,1,0:T(8,128)(2,1)} %param.11) | copy-start | bytes 12582916
  19.9 10.4 %collective-permute-start.11 = (f32[2,256,256]{2,1,0:T(8,128)S(1)}, f32[2,256,256]{2,1,0:T(8,128)S(1)}, u32[]{:S(2)}, u32[]{:S(2)}) collective-permute-start(f32[2,256,256]{2,1,0:T(8,128)S(1)} %tie.2.top_ref), channel_id=1, source_target_pairs={{1,0},{2,1},{3,2},{5,4},{6,5},{7,6},{9,8},{10,9},{11,10},{13,12},{... | collective-permute-start | bytes 1572872 | tf_op jit(solution)/shard_map/ppermute | solution.py:19
  34.7 42.3 %collective-permute-start.13 = (f32[2,2,256,128]{3,2,1,0:T(8,128)S(1)}, f32[2,2,256,128]{3,2,1,0:T(8,128)S(1)}, u32[]{:S(2)}, u32[]{:S(2)}) collective-permute-start(f32[2,2,256,128]{3,2,1,0:T(8,128)S(1)} %get-tuple-element.27), channel_id=1, source_target_pairs={{0,1},{1,2},{2,3},{4,5},{5,6},{6,7},{8,9},{9,10},{10,11},{12,13},{... | collective-permute-start | bytes 1572872 | tf_op jit(solution)/shard_map/ppermute | solution.py:19
  62.5 1.6 %copy-start.1 = (f32[2,4,768,128]{3,2,1,0:T(8,128)}, f32[2,4,768,128]{3,2,1,0:T(8,128)S(1)}, u32[]{:S(2)}) copy-start(f32[2,4,768,128]{3,2,1,0:T(8,128)S(1)} %get-tuple-element.24.update) | copy-start | bytes 9437188
  64.2 64.1 %collective-permute-start.12 = (f32[2,4,256,128]{3,2,1,0:T(8,128)}, f32[2,4,256,128]{3,2,1,0:T(8,128)S(1)}, u32[]{:S(2)}, u32[]{:S(2)}) collective-permute-start(f32[2,4,256,128]{3,2,1,0:T(8,128)} %get-tuple-element.25), channel_id=1, source_target_pairs={{0,1},{1,2},{2,3},{4,5},{5,6},{6,7},{8,9},{9,10},{10,11},{12,13},{... | collective-permute-start | bytes 3145736 | tf_op jit(solution)/shard_map/ppermute | solution.py:19
  68.1 60.2 %collective-permute-start.15 = (f32[2,2,256,128]{3,2,1,0:T(8,128)}, f32[2,2,256,128]{3,2,1,0:T(8,128)}, u32[]{:S(2)}, u32[]{:S(2)}) collective-permute-start(f32[2,2,256,128]{3,2,1,0:T(8,128)} %get-tuple-element.29), channel_id=1, source_target_pairs={{0,4},{4,8},{8,12},{12,16},{16,20},{20,24},{24,28},{1,5},{5,9},{9,... | collective-permute-start | bytes 1572872 | tf_op jit(solution)/shard_map/ppermute | solution.py:19
  77.9 50.4 %collective-permute-start.14 = (f32[2,2,256,128]{3,2,1,0:T(8,128)}, f32[2,2,256,128]{3,2,1,0:T(8,128)}, u32[]{:S(2)}, u32[]{:S(2)}) collective-permute-start(f32[2,2,256,128]{3,2,1,0:T(8,128)} %add.34), channel_id=1, source_target_pairs={{0,4},{4,8},{8,12},{12,16},{16,20},{20,24},{24,28},{1,5},{5,9},{9,... | collective-permute-start | bytes 1572872 | tf_op jit(solution)/shard_map/ppermute | solution.py:19
  81.1 1.7 %collective-permute-start = (f32[256,256]{1,0:T(8,128)S(1)}, f32[256,256]{1,0:T(8,128)}, u32[]{:S(2)}, u32[]{:S(2)}) collective-permute-start(f32[256,256]{1,0:T(8,128)S(1)} %select_bitcast_fusion), channel_id=1, source_target_pairs={{0,1},{1,0},{2,3},{3,2},{4,5},{5,4},{6,7},{7,6},{8,9},{9,8},{10,11... | collective-permute-start | bytes 786440 | tf_op jit(solution)/shard_map/cond/branch_1_fun/ppermute | solution.py:290
  84.7 5.7 %collective-permute-start.1 = (f32[128,256]{1,0:T(8,128)}, f32[128,256]{1,0:T(8,128)S(1)}, u32[]{:S(2)}, u32[]{:S(2)}) collective-permute-start(f32[128,256]{1,0:T(8,128)} %slice_select_fusion), channel_id=1, source_target_pairs={{0,2},{1,3},{2,0},{3,1},{4,6},{5,7},{6,4},{7,5},{8,10},{9,11},{10,... | collective-permute-start | bytes 393224 | tf_op jit(solution)/shard_map/cond/branch_1_fun/ppermute | solution.py:290
  90.5 8.8 %collective-permute-start.2 = (f32[64,256]{1,0:T(8,128)S(1)}, f32[64,256]{1,0:T(8,128)S(1)}, u32[]{:S(2)}, u32[]{:S(2)}) collective-permute-start(f32[64,256]{1,0:T(8,128)S(1)} %slice_select_fusion.1), channel_id=1, source_target_pairs={{0,16},{4,20},{8,24},{12,28},{16,0},{20,4},{24,8},{28,12},{1,17},{... | collective-permute-start | bytes 196616 | tf_op jit(solution)/shard_map/cond/branch_1_fun/ppermute | solution.py:290
  99.3 6.4 %collective-permute-start.3 = (f32[64,256]{1,0:T(8,128)S(1)}, f32[64,256]{1,0:T(8,128)S(1)}, u32[]{:S(2)}, u32[]{:S(2)}) collective-permute-start(f32[64,256]{1,0:T(8,128)S(1)} %select_add_fusion.1), channel_id=1, source_target_pairs={{0,8},{4,12},{8,0},{12,4},{16,24},{20,28},{24,16},{28,20},{1,9},{5... | collective-permute-start | bytes 196616 | tf_op jit(solution)/shard_map/cond/branch_1_fun/ppermute | solution.py:290
  105.7 9.4 %collective-permute-start.4 = (f32[64,256]{1,0:T(8,128)S(1)}, f32[64,256]{1,0:T(8,128)S(1)}, u32[]{:S(2)}, u32[]{:S(2)}) collective-permute-start(f32[64,256]{1,0:T(8,128)S(1)} %add.31), channel_id=1, source_target_pairs={{0,4},{4,0},{8,12},{12,8},{16,20},{20,16},{24,28},{28,24},{1,5},{5... | collective-permute-start | bytes 196616 | tf_op jit(solution)/shard_map/cond/branch_1_fun/ppermute | solution.py:290
  115.1 5.7 %collective-permute-start.5 = (f32[64,256]{1,0:T(8,128)S(1)}, f32[64,256]{1,0:T(8,128)S(1)}, u32[]{:S(2)}, u32[]{:S(2)}) collective-permute-start(f32[64,256]{1,0:T(8,128)S(1)} %add_multiply_fusion), channel_id=1, source_target_pairs={{0,16},{4,20},{8,24},{12,28},{16,0},{20,4},{24,8},{28,12},{1,17},{... | collective-permute-start | bytes 196616 | tf_op jit(solution)/shard_map/cond/branch_1_fun/ppermute | solution.py:290
  120.8 5.0 %collective-permute-start.6 = (f32[128,256]{1,0:T(8,128)S(1)}, f32[128,256]{1,0:T(8,128)S(1)}, u32[]{:S(2)}, u32[]{:S(2)}) collective-permute-start(f32[128,256]{1,0:T(8,128)S(1)} %maximum_select_fusion.2), channel_id=1, source_target_pairs={{0,2},{1,3},{2,0},{3,1},{4,6},{5,7},{6,4},{7,5},{8,10},{9,11},{10,... | collective-permute-start | bytes 393224 | tf_op jit(solution)/shard_map/cond/branch_1_fun/ppermute | solution.py:290
  125.9 1.6 %collective-permute-start.7 = (f32[256,256]{1,0:T(8,128)S(1)}, f32[256,256]{1,0:T(8,128)S(1)}, u32[]{:S(2)}, u32[]{:S(2)}) collective-permute-start(f32[256,256]{1,0:T(8,128)S(1)} %maximum_select_fusion.1), channel_id=1, source_target_pairs={{0,1},{1,0},{2,3},{3,2},{4,5},{5,4},{6,7},{7,6},{8,9},{9,8},{10,11... | collective-permute-start | bytes 786440 | tf_op jit(solution)/shard_map/cond/branch_1_fun/ppermute | solution.py:290
  128.3 1.9 %copy-start.2 = (f32[2,4,768,128]{3,2,1,0:T(8,128)S(1)}, f32[2,4,768,128]{3,2,1,0:T(8,128)}, u32[]{:S(2)}) copy-start(f32[2,4,768,128]{3,2,1,0:T(8,128)} %copy-done.1) | copy-start | bytes 9437188
  (1 other events, 1.0 us)

commit v3 on v2

--- a/solution.py
+++ b/solution.py
@@ -10,7 +10,7 @@
 
 LANES = 128
 STEP = 32
-GROUP = 2
+GROUP = 4
 
 
 def passed_along(block, axis, distance):
@@ -100,21 +100,22 @@
                     xs[0, rows, cols] = up + low
                     xs[1, rows, cols] = up - low
 
-    def group_step(step, carry):
-        slots = [order_ref[GROUP * step + i] for i in range(GROUP)]
-        for which in range(GROUP):
+    def run_group(count, first, all_live):
+        wide = slice(0, count * size)
+        slots = [order_ref[first + i] for i in range(count)]
+        for which in range(count):
             read(which, slots[which])
-        near = [dot(mats[parity], xs[parity]).astype(bf16) for parity in range(2)]
+        near = [dot(mats[parity], xs[parity, :, wide]).astype(bf16) for parity in range(2)]
         folds = [[], []]
-        for which in range(GROUP):
+        for which in range(count):
             for parity in range(2):
                 left = near[parity][:, which * size:which * size + half]
                 right = near[parity][:, which * size + half:(which + 1) * size]
                 for sign, both in enumerate((left + right, left - right)):
                     folds[sign].append(jnp.concatenate([both[:half], both[half:]], axis=1))
         for sign in range(2):
-            far[sign] = dot(jnp.concatenate(folds[sign], axis=0), mats[2 + sign])
-        for which in range(GROUP):
+            far[sign, wide, :] = dot(jnp.concatenate(folds[sign], axis=0), mats[2 + sign])
+        for which in range(count):
             for at in range(0, size, STEP):
                 rows = slice(which * size + at, which * size + at + STEP)
                 for block in range(2):
@@ -126,28 +127,28 @@
                     cols = slice(which * size + block * LANES, which * size + (block + 1) * LANES)
                     gs[at // half, down:down + STEP, cols] = (re * ratio).astype(bf16)
                     gs[at // half, half + down:half + down + STEP, cols] = (im * ratio).astype(bf16)
-        even = dot(mats[4], gs[0])
-        odd = dot(mats[5], gs[1])
+        even = dot(mats[4], gs[0, :, wide])
+        odd = dot(mats[5], gs[1, :, wide])
         back = (even + odd).astype(bf16), (even - odd).astype(bf16)
         sums = []
         for parity in range(2):
             parts = []
-            for which in range(GROUP):
+            for which in range(count):
                 cols = slice(which * size + parity * half, which * size + (parity + 1) * half)
                 for value in back:
                     parts.append(jnp.concatenate([value[:half, cols], value[half:, cols]], axis=1))
             sums.append(dot(jnp.concatenate(parts, axis=0), mats[6 + parity]))
         places = [place(slot) for slot in slots]
-        weights = [None] + [jnp.where(GROUP * step + i < found, 1.0, 0.0).astype(jnp.float32) for i in range(1, GROUP)]
+        weights = [None] * count if all_live else [None] + [jnp.where(first + i < found, 1.0, 0.0).astype(jnp.float32) for i in range(1, count)]
         for at in range(0, size, STEP):
             rows = slice(at, at + STEP)
-            terms = [[[], []] for _ in range(GROUP)]
+            terms = [[[], []] for _ in range(count)]
             for block in range(2):
                 cols = slice(block * LANES, (block + 1) * LANES)
                 probe_re = probe_ref[0, rows, cols]
                 probe_im = probe_ref[1, rows, cols]
                 total = None
-                for which in range(GROUP):
+                for which in range(count):
                     patch_re = patch[which, 0, rows, cols]
                     patch_im = patch[which, 1, rows, cols]
                     delta = []
@@ -155,7 +156,7 @@
                         a = sums[0][which * size + at:which * size + at + STEP, plane * half:(plane + 1) * half]
                         b = sums[1][which * size + at:which * size + at + STEP, plane * half:(plane + 1) * half]
                         value = (a + b if block == 0 else a - b) - value
-                        delta.append(value if which == 0 else value * weights[which])
+                        delta.append(value if weights[which] is None else value * weights[which])
                     shift = places[which][2]
                     terms[which][0].append(pltpu.roll(probe_re * delta[0] + probe_im * delta[1], shift, 1))
                     terms[which][1].append(pltpu.roll(probe_re * delta[1] - probe_im * delta[0], shift, 1))
@@ -163,7 +164,7 @@
                     total = own_sum if total is None else (total[0] + own_sum[0], total[1] + own_sum[1])
                 probe_sum[0, rows, cols] += total[0]
                 probe_sum[1, rows, cols] += total[1]
-            for which in range(GROUP):
+            for which in range(count):
                 row, base, shift = places[which]
                 own = lax.broadcasted_iota(jnp.int32, (STEP, LANES), 1) >= shift
                 for plane in range(2):
@@ -171,9 +172,17 @@
                     update[plane, base, pl.ds(row + at, STEP), :] += jnp.where(own, first, 0.0)
                     update[plane, base + 1, pl.ds(row + at, STEP), :] += jnp.where(own, second, first)
                     update[plane, base + 2, pl.ds(row + at, STEP), :] += jnp.where(own, 0.0, second)
+
+    def whole_group(step, carry):
+        run_group(GROUP, step * GROUP, True)
         return carry
 
-    lax.fori_loop(0, (found + GROUP - 1) // GROUP, group_step, 0)
+    def pair(step, carry):
+        run_group(2, found // GROUP * GROUP + step * 2, False)
+        return carry
+
+    lax.fori_loop(0, found // GROUP, whole_group, 0)
+    lax.fori_loop(0, (found % GROUP + 1) // 2, pair, 0)
 
 
 def put(into, row, col, value):
@@ -183,13 +192,17 @@
 
 
 def inner_kernel(rows_ref, cols_ref, count_ref, block_ref, probe_ref, amps_ref, mats,
-                 update, probe_sum, amp_ref, order_ref, field, *scratch):
+                 update, probe_sum, amp_ref, scale_ref, order_ref, field, *scratch):
     size = probe_ref.shape[1]
     rows_here, cols_here = block_ref.shape[1:]
     put(field, 0, 0, block_ref)
     update[...] = jnp.zeros_like(update)
     probe_sum[...] = jnp.zeros_like(probe_sum)
-    live = count_ref[0]
+    probe_re = probe_ref[0]
+    probe_im = probe_ref[1]
+    power = jnp.mean(probe_re * probe_re + probe_im * probe_im) + 1e-06
+    scale_ref[...] = jnp.ones_like(scale_ref) / power
+    live = count_ref[0, 0]
     total = rows_ref.shape[0]
     batch = math.gcd(4, total)
 
@@ -209,9 +222,27 @@
     run_slots(found, order_ref, rows_ref, cols_ref, probe_ref, amp_ref, mats, field, update, probe_sum, scratch)
 
 
+def lower_kernel(rows_ref, cols_ref, count_ref, block_ref, lower_ref, probe_ref, amp_ref, mats, update_in, probe_in,
+                 update, probe_sum, order_ref, field, *scratch):
+    size = probe_ref.shape[1]
+    rows_here, cols_here = block_ref.shape[1:]
+    put(field, 0, 0, block_ref)
+    put(field, rows_here, 0, lower_ref)
+    update[:, :, :rows_here, :] = update_in[...]
+    update[:, :, rows_here:, :] = jnp.zeros((2, cols_here // LANES, size, LANES), jnp.float32)
+    probe_sum[...] = probe_in[...]
+    live = count_ref[0, 0]
+
+    def keep(slot):
+        return (slot < live) & (cols_ref[slot] < cols_here - size) & (rows_ref[slot] > rows_here - size)
+
+    found = collect(keep, rows_ref.shape[0], order_ref)
+    run_slots(found, order_ref, rows_ref, cols_ref, probe_ref, amp_ref, mats, field, update, probe_sum, scratch)
+
+
 def right_kernel(rows_ref, cols_ref, count_ref, block_ref, lower_ref, top_ref, side_ref, corner_ref,
                  probe_ref, amp_ref, mats, update_in, probe_in,
-                 update_out, probe_sum, top_out, side_out, corner_out, order_ref, field, update, *scratch):
+                 own_out, low_out, top_out, side_out, corner_out, kept_out, given_out, alive_ref, order_ref, field, update, probe_sum, *scratch):
     size = probe_ref.shape[1]
     rows_here, cols_here = block_ref.shape[1:]
     edge = cols_here // LANES
@@ -220,35 +251,34 @@
     put(field, 0, cols_here, top_ref)
     put(field, size, cols_here, side_ref)
     put(field, rows_here, cols_here, corner_ref)
-    update[:, :edge, :rows_here, :] = update_in[...]
-    update[:, :edge, rows_here:, :] = jnp.zeros((2, edge, size, LANES), jnp.float32)
+    update[:, :edge, :, :] = update_in[...]
     update[:, edge:, :, :] = jnp.zeros((2, size // LANES, rows_here + size, LANES), jnp.float32)
     probe_sum[...] = probe_in[...]
-    live = count_ref[0]
+    live = count_ref[0, 0]
     found = collect(lambda slot: (slot < live) & (cols_ref[slot] >= cols_here - size), rows_ref.shape[0], order_ref)
     run_slots(found, order_ref, rows_ref, cols_ref, probe_ref, amp_ref, mats, field, update, probe_sum, scratch)
-    update_out[...] = update[:, :edge, :, :]
+    corner_out[...] = update[:, edge:, rows_here:, :]
+    side_out[...] = update[:, edge:, size:rows_here, :]
     top_out[...] = update[:, edge:, :size, :]
-    side_out[...] = update[:, edge:, size:rows_here, :]
-    corner_out[...] = update[:, edge:, rows_here:, :]
-
-
-def lower_kernel(rows_ref, cols_ref, count_ref, block_ref, lower_ref, probe_ref, amp_ref, mats, update_in, probe_in,
-                 update, low_out, probe_sum, order_ref, field, *scratch):
-    size = probe_ref.shape[1]
-    rows_here, cols_here = block_ref.shape[1:]
-    put(field, 0, 0, block_ref)
-    put(field, rows_here, 0, lower_ref)
-    update[...] = update_in[...]
-    probe_sum[...] = probe_in[...]
-    live = count_ref[0]
-
-    def keep(slot):
-        return (slot < live) & (cols_ref[slot] < cols_here - size) & (rows_ref[slot] > rows_here - size)
-
-    found = collect(keep, rows_ref.shape[0], order_ref)
-    run_slots(found, order_ref, rows_ref, cols_ref, probe_ref, amp_ref, mats, field, update, probe_sum, scratch)
-    low_out[...] = update[:, :, rows_here:, :]
+    low_out[...] = update[:, :edge, rows_here:, :]
+    own_out[...] = update[:, :edge, :rows_here, :]
+    half = lax.rem(lax.axis_index("tile"), 2)
+    alive_ref[0] = live
+    kept_out[...] = probe_sum[half]
+    given_out[...] = probe_sum[1 - half]
+
+
+def cut_kernel(block, top_out, side_out, low_out, sems):
+    size = top_out.shape[1]
+    copies = [
+        pltpu.make_async_copy(block.at[:, :size, :size], top_out, sems.at[0]),
+        pltpu.make_async_copy(block.at[:, size:, :size], side_out, sems.at[1]),
+        pltpu.make_async_copy(block.at[:, :size, :], low_out, sems.at[2]),
+    ]
+    for copy in copies:
+        copy.start()
+    for copy in copies:
+        copy.wait()
 
 
 def tie_kernel(value_in, other_in, value_out):
@@ -268,18 +298,15 @@
     )(value, other)
 
 
-def finish_kernel(block_ref, update, low_ref, top_ref, side_ref, probe_ref, out_ref):
-    size = probe_ref.shape[1]
-    rows_here, cols_here = block_ref.shape[1:]
-    probe_re = probe_ref[0]
-    probe_im = probe_ref[1]
-    scale = 1.0 / (jnp.mean(probe_re * probe_re + probe_im * probe_im) + 1e-06)
+def finish_kernel(block_ref, update, low_ref, top_ref, side_ref, scale_ref, out_ref):
+    size = low_ref.shape[2]
+    scale = scale_ref[0:1, :]
     for plane in range(2):
-        for block in range(cols_here // LANES):
+        for block in range(update.shape[1]):
             cols = slice(block * LANES, (block + 1) * LANES)
             top = update[plane, block, :size, :] + low_ref[plane, block]
-            side = update[plane, block, size:rows_here, :]
-            if block < size // LANES:
+            side = update[plane, block, size:, :]
+            if block < top_ref.shape[1]:
                 top = top + top_ref[plane, block]
                 side = side + side_ref[plane, block]
             out_ref[plane, :size, cols] = block_ref[plane, :size, cols] + top * scale
@@ -322,12 +349,9 @@
     mats = jnp.asarray(dft_blocks(size))
     slot_rows = corner_rows.reshape(slots)
     slot_cols = corner_cols.reshape(slots)
-    live_count = counts.reshape(1)
+    live_count = counts
     amps = amplitudes.reshape(slots, size, size)
 
-    right_top = passed_along(object_field[:, :size, :size], "pos", -1)
-    right_side = passed_along(object_field[:, size:, :size], "pos", -1)
-    lower = passed_along(object_field[:, :size, :], "tile", -1)
     smem = pl.BlockSpec(memory_space=pltpu.SMEM)
     vmem = pl.BlockSpec(memory_space=pltpu.VMEM)
 
@@ -343,54 +367,66 @@
             pltpu.VMEM((2, size, GROUP * size), jnp.bfloat16),
         ]
 
-    def call(kernel, name, outs, held, *arrays):
+    def call(kernel, name, mib, outs, held, *arrays, flags=0):
         return pl.pallas_call(
             kernel,
             out_shape=outs,
             in_specs=[smem] * 3 + [vmem] * len(arrays),
-            out_specs=[vmem] * len(outs),
-            scratch_shapes=scratch(*held),
-            compiler_params=params,
+            out_specs=[vmem] * (len(outs) - flags) + [smem] * flags,
+            scratch_shapes=[*scratch(*held[:3])[:1 + held[2]], *held[3:], *scratch(*held[:3])[1 + held[2]:]],
+            compiler_params=pltpu.CompilerParams(vmem_limit_bytes=mib * 1024 * 1024),
             cost_estimate=pl.CostEstimate(
                 flops=slots // 4 * 32 * size**3, bytes_accessed=8 * size * size * slots, transcendentals=0),
             name=name,
         )(slot_rows, slot_cols, live_count, *arrays)
 
-    params = pltpu.CompilerParams(vmem_limit_bytes=24 * 1024 * 1024)
     edge = cols_here // LANES
     rim = size // LANES
     plane = f32(2, size, size)
-
-    update, probe_sum, amps = call(
-        inner_kernel, "inner_slots", [f32(2, edge, rows_here, LANES), plane, jax.ShapeDtypeStruct(amps.shape, amps.dtype)],
+    anywhere = pl.BlockSpec(memory_space=pl.ANY)
+    top_cut, side_cut, low_cut = pl.pallas_call(
+        cut_kernel,
+        out_shape=(plane, f32(2, rows_here - size, size), f32(2, size, cols_here)),
+        in_specs=[anywhere],
+        out_specs=(anywhere,) * 3,
+        scratch_shapes=[pltpu.SemaphoreType.DMA((3,))],
+        compiler_params=pltpu.CompilerParams(vmem_limit_bytes=1024 * 1024),
+        name="cut",
+    )(object_field)
+    right_top = passed_along(top_cut, "pos", -1)
+    right_side = passed_along(side_cut, "pos", -1)
+    lower = passed_along(low_cut, "tile", -1)
+
+    tile_steps = masks_of("tile")
+    pos_steps = masks_of("pos")[::-1]
+    update, probe_sum, amps, scale = call(
+        inner_kernel, "inner_slots", 20,
+        [f32(2, edge, rows_here, LANES), plane, jax.ShapeDtypeStruct(amps.shape, amps.dtype), f32(8, LANES)],
         (edge, rows_here, 1), object_field, probe, amps, mats)
 
     right_top = tie(right_top, probe_sum)
     corner = passed_along(right_top, "tile", -1)
 
-    update, probe_sum, top_part, side_part, corner_part = call(
-        right_kernel, "right_slots",
-        [f32(2, edge, rows_here + size, LANES), plane, f32(2, rim, size, LANES),
-         f32(2, rim, rows_here - size, LANES), f32(2, rim, size, LANES)],
-        (edge + rim, rows_here + size, 2),
-        object_field, lower, right_top, right_side, corner, probe, amps, mats, update, probe_sum)
-
-    corner_back = passed_along(corner_part, "tile", 1)
-    side_back = passed_along(side_part, "pos", 1)
-
-    update, low_part, probe_sum = call(
-        lower_kernel, "lower_slots",
-        [f32(2, edge, rows_here + size, LANES), f32(2, edge, size, LANES), plane],
+    update, probe_sum = call(
+        lower_kernel, "lower_slots", 20, [f32(2, edge, rows_here + size, LANES), plane],
         (edge, rows_here + size, 1), object_field, lower, probe, amps, mats, update, probe_sum)
 
-    low_back = passed_along(low_part, "tile", 1)
-    top_back = passed_along(top_part + tie(corner_back, probe_sum), "pos", 1)
-
-    tile_steps = masks_of("tile")
-    pos_steps = masks_of("pos")[::-1]
-
-    def sum_all(value):
-        for step in tile_steps + pos_steps[:-2]:
+    own_part, low_part, top_part, side_part, corner_part, kept, given, alive = call(
+        right_kernel, "right_slots", 26,
+        [f32(2, edge, rows_here, LANES), f32(2, edge, size, LANES), f32(2, rim, size, LANES),
+         f32(2, rim, rows_here - size, LANES), f32(2, rim, size, LANES), f32(size, size), f32(size, size),
+         jax.ShapeDtypeStruct((1,), jnp.int32)],
+        (edge + rim, rows_here + size, 2, pltpu.VMEM((2, size, size), jnp.float32)),
+        object_field, lower, right_top, right_side, corner, probe, amps, mats, update, probe_sum, flags=1)
+
+    def sum_first(kept, given):
+        value = kept + partner(given, *tile_steps[0])
+        for step in tile_steps[1:]:
+            value = halve(value, *step)
+        return value
+
+    def sum_rest(value):
+        for step in pos_steps[:-2]:
             value = halve(value, *step)
         for step in pos_steps[-2:]:
             value = value + partner(value, *step)
@@ -399,16 +435,22 @@
             value = rejoin(value, *step)
         return value
 
-    probe_grad = lax.cond(live_count[0] >= 1, sum_all, jnp.zeros_like, probe_sum.reshape(2 * size, size))
+    corner_back = passed_along(corner_part, "tile", 1)
+    side_back = passed_along(side_part, "pos", 1)
+    low_back = passed_along(low_part, "tile", 1)
+    share = 2 * size // lax.axis_size("tile")
+    summed = lax.cond(alive[0] >= 1, sum_first, lambda kept, given: kept[:share], kept, given)
+    top_back = passed_along(top_part + tie(corner_back, summed), "pos", 1)
+    probe_grad = lax.cond(alive[0] >= 1, sum_rest, lambda v: jnp.zeros((2 * size, size), jnp.float32), summed)
 
     object_new = pl.pallas_call(
         finish_kernel,
         out_shape=f32(2, rows_here, cols_here),
         in_specs=[vmem] * 6,
         out_specs=vmem,
-        compiler_params=params,
+        compiler_params=pltpu.CompilerParams(vmem_limit_bytes=8 * 1024 * 1024),
         name="finish",
-    )(object_field, update, low_back, top_back, side_back, probe)
+    )(object_field, own_part, low_back, top_back, side_back, scale)
     return (object_new, probe_grad.reshape(2, size, size))
 
 

time: 133 us -> 129 us (0.970)
  the two profiles are of different devices: /device:TPU:0 before, /device:TPU:31 now
where the time goes in v3:
time: 129 us; the launch traced here: 127 us
  waiting for transfers between devices  46.4 us (36%)
  starting transfers between devices  46.1 us (36%)
  Pallas kernels  20.2 us (16%)
  local copies, waits for them, and re-layouts  9.05 us (7%)
  other arithmetic  2.81 us (2%)
  between operations  2.19 us (2%)
    ppermute x8, waiting for transfers between devices, partner(): lax.ppermute(block, axis, [(i, i ^ mask) for i in range(lax.axis_size(axi...  45.2 us
    ppermute x8, starting transfers between devices, partner(): lax.ppermute(block, axis, [(i, i ^ mask) for i in range(lax.axis_size(axi...  31.6 us
    pallas_call x3, Pallas kernels, call(): pl.pallas_call(kernel, out_shape=outs, in_specs=[smem] * 3 + [vmem] * len...  16.8 us
    ppermute x8, starting transfers between devices, passed_along(): return lax.ppermute(block, axis, route)  14.4 us
    unnamed x22, local copies, waits for them, and re-layouts  9.05 us
    pallas_call x1, Pallas kernels, shards(): pl.pallas_call(finish_kernel, out_shape=f32(2, rows_here, cols_here), in_...  3.15 us
  transfers between devices with their start and end apart: 16, of which 9 were waited for; matrix products, arithmetic and copies ran while one was open for 2% of the time, Pallas kernels for 9%

profile of v3, /device:TPU:31, one launch (start us, length us, event | category | flops | bytes accessed | tf_op | source)
XLA Modules:
  0.0 126.9 jit_solution(9203309534311918685)
XLA Ops:
  0.6 1.6 %copy-done = f32[2,512,512]{2,1,0:T(8,128)S(1)} copy-done((f32[2,512,512]{2,1,0:T(8,128)S(1)}, f32[2,512,512]{2,1,0:T(8,128)}, u32[]{:S(2)}) %copy-start) | copy-done | bytes 2097176
  2.5 2.8 %collective-permute-start.8 = (f32[2,256,512]{2,1,0:T(8,128)S(1)}, f32[2,256,512]{2,1,0:T(8,128)S(1)}, u32[]{:S(2)}, u32[]{:S(2)}) collective-permute-start(f32[2,256,512]{2,1,0:T(8,128)S(1)} %get-tuple-element.34), channel_id=1, source_target_pairs={{1,0},{2,1},{3,2},{5,4},{6,5},{7,6},{9,8},{10,9},{11,10},{13,12},{... | collective-permute-start | bytes 3145736 | tf_op jit(solution)/shard_map/ppermute | solution.py:19
  5.3 2.2 %collective-permute-start.9 = (f32[2,256,256]{2,1,0:T(8,128)S(1)}, f32[2,256,256]{2,1,0:T(8,128)S(1)}, u32[]{:S(2)}, u32[]{:S(2)}) collective-permute-start(f32[2,256,256]{2,1,0:T(8,128)S(1)} %get-tuple-element.35), channel_id=1, source_target_pairs={{4,0},{8,4},{12,8},{16,12},{20,16},{24,20},{28,24},{5,1},{9,5},{13... | collective-permute-start | bytes 1572872 | tf_op jit(solution)/shard_map/ppermute | solution.py:19
  7.5 3.0 %collective-permute-start.10 = (f32[2,256,256]{2,1,0:T(8,128)S(1)}, f32[2,256,256]{2,1,0:T(8,128)S(1)}, u32[]{:S(2)}, u32[]{:S(2)}) collective-permute-start(f32[2,256,256]{2,1,0:T(8,128)S(1)} %get-tuple-element.37), channel_id=1, source_target_pairs={{4,0},{8,4},{12,8},{16,12},{20,16},{24,20},{28,24},{5,1},{9,5},{13... | collective-permute-start | bytes 1572872 | tf_op jit(solution)/shard_map/ppermute | solution.py:19
  11.2 2.2 %copy-done.4 = bf16[1,1,32,256,256]{4,3,2,1,0:T(8,128)(2,1)S(1)} copy-done((bf16[1,1,32,256,256]{4,3,2,1,0:T(8,128)(2,1)S(1)}, bf16[1,1,32,256,256]{4,3,2,1,0:T(8,128)(2,1)}, u32[]{:S(2)}) %copy-start.4) | copy-done | bytes 4194328
  15.7 6.1 %inner_slots.1 = (f32[2,4,512,128]{3,2,1,0:T(8,128)S(1)}, f32[2,256,256]{2,1,0:T(8,128)S(1)}, bf16[32,256,256]{2,1,0:T(8,128)(2,1)S(1)}, f32[8,128]{1,0:T(8,128)S(1)}) custom-call(s32[32]{0:T(128)S(1)} %bitcast.6, s32[32]{0:T(128)S(1)} %bitcast.9, s32[1,1]{1,0:T(1,128)S(6)} %copy.17.count_ref, f32[2,512,512]{2,1,0:T(8,128)S(1)} %copy-done.1, ...), custom_call_target="tpu_custom_call" | custom-call | flops 4294967296 | bytes 16777216 | tf_op jit(solution)/shard_map/inner_slots/pallas_call | solution.py:371
  21.8 1.3 %collective-permute-start.11 = (f32[2,256,256]{2,1,0:T(8,128)S(1)}, f32[2,256,256]{2,1,0:T(8,128)S(1)}, u32[]{:S(2)}, u32[]{:S(2)}) collective-permute-start(f32[2,256,256]{2,1,0:T(8,128)S(1)} %tie.2.top_ref), channel_id=1, source_target_pairs={{1,0},{2,1},{3,2},{5,4},{6,5},{7,6},{9,8},{10,9},{11,10},{13,12},{... | collective-permute-start | bytes 1572872 | tf_op jit(solution)/shard_map/ppermute | solution.py:19
  23.2 5.7 %lower_slots.1 = (f32[2,4,768,128]{3,2,1,0:T(8,128)S(1)}, f32[2,256,256]{2,1,0:T(8,128)S(1)}) custom-call(s32[32]{0:T(128)S(1)} %bitcast.7, s32[32]{0:T(128)S(1)} %bitcast.10, s32[1,1]{1,0:T(1,128)S(6)} %copy.17.count_ref, f32[2,512,512]{2,1,0:T(8,128)S(1)} %copy-done.1, f32[2,256,512]{2,1,0:T(8,128)S(1)} %collective-permute-done.8.lower_ref, ...), custom_call_target="tpu_custom_call" | custom-call | flops 4294967296 | bytes 16777216 | tf_op jit(solution)/shard_map/lower_slots/pallas_call | solution.py:371
  30.1 5.0 %right_slots.1 = (f32[2,4,512,128]{3,2,1,0:T(8,128)S(1)}, f32[2,4,256,128]{3,2,1,0:T(8,128)}, f32[2,2,256,128]{3,2,1,0:T(8,128)S(1)}, f32[2,2,256,128]{3,2,1,0:T...) custom-call(s32[32]{0:T(128)S(1)} %bitcast.8, s32[32]{0:T(128)S(1)} %bitcast.11, ...), custom_call_target="tpu_custom_call" | custom-call | flops 4294967296 | bytes 16777216 | tf_op jit(solution)/shard_map/right_slots/pallas_call | solution.py:371
  41.0 31.4 %conditional.2 = (f32[128,256]{1,0:T(8,128)S(1)}) conditional(s32[]{:T(128)} %bitcast.4, f32[256,256]{1,0:T(8,128)S(1)} %get-tuple-element.47, (f32[256,256]{1,0:T(8,128)}, f32[256,256]{1,0:T(8,128)S(1)}) %tuple.22), branch_computations={%region_0.0_spmd, %region_1.2_spmd} | conditional | flops 163869 | bytes 3277178 | solution.py:442
  41.0 5.2 %collective-permute-start = (f32[256,256]{1,0:T(8,128)}, f32[256,256]{1,0:T(8,128)}, u32[]{:S(2)}, u32[]{:S(2)}) collective-permute-start(f32[256,256]{1,0:T(8,128)} %get-tuple-element.14), channel_id=1, source_target_pairs={{0,1},{1,0},{2,3},{3,2},{4,5},{5,4},{6,7},{7,6},{8,9},{9,8},{10,11... | collective-permute-start | bytes 786440 | tf_op jit(solution)/shard_map/cond/branch_1_fun/ppermute | solution.py:317
  46.2 1.5 %collective-permute-done = f32[256,256]{1,0:T(8,128)} collective-permute-done((f32[256,256]{1,0:T(8,128)}, f32[256,256]{1,0:T(8,128)}, u32[]{:S(2)}, u32[]{:S(2)}) %collective-permute-start) | collective-permute-done | bytes 262176 | tf_op jit(solution)/shard_map/cond/branch_1_fun/ppermute | solution.py:317
  48.7 10.5 %collective-permute-start.1 = (f32[128,256]{1,0:T(8,128)S(1)}, f32[128,256]{1,0:T(8,128)S(1)}, u32[]{:S(2)}, u32[]{:S(2)}) collective-permute-start(f32[128,256]{1,0:T(8,128)S(1)} %slice_select_fusion), channel_id=1, source_target_pairs={{0,2},{1,3},{2,0},{3,1},{4,6},{5,7},{6,4},{7,5},{8,10},{9,11},{10,... | collective-permute-start | bytes 393224 | tf_op jit(solution)/shard_map/cond/branch_1_fun/ppermute | solution.py:317
  59.3 13.1 %collective-permute-done.1 = f32[128,256]{1,0:T(8,128)S(1)} collective-permute-done((f32[128,256]{1,0:T(8,128)S(1)}, f32[128,256]{1,0:T(8,128)S(1)}, u32[]{:S(2)}, u32[]{:S(2)}) %collective-permute-start.1) | collective-permute-done | bytes 131104 | tf_op jit(solution)/shard_map/cond/branch_1_fun/ppermute | solution.py:317
  74.6 47.5 %conditional.3 = (f32[2,256,256]{2,1,0:T(8,128)}) conditional(s32[]{:T(128)} %bitcast.4, () %tuple.23, f32[128,256]{1,0:T(8,128)S(1)} %get-tuple-element.51.other_in), branch_computations={%region_2.3_spmd, %region_3.4_spmd} | conditional | flops 786496 | bytes 5309303 | solution.py:444
  74.6 11.0 %collective-permute-start.2 = (f32[64,256]{1,0:T(8,128)S(1)}, f32[64,256]{1,0:T(8,128)S(1)}, u32[]{:S(2)}, u32[]{:S(2)}) collective-permute-start(f32[64,256]{1,0:T(8,128)S(1)} %slice_select_fusion.1), channel_id=1, source_target_pairs={{0,16},{4,20},{8,24},{12,28},{16,0},{20,4},{24,8},{28,12},{1,17},{... | collective-permute-start | bytes 196616 | tf_op jit(solution)/shard_map/cond/branch_1_fun/ppermute | solution.py:317
  85.7 14.7 %collective-permute-done.2 = f32[64,256]{1,0:T(8,128)S(1)} collective-permute-done((f32[64,256]{1,0:T(8,128)S(1)}, f32[64,256]{1,0:T(8,128)S(1)}, u32[]{:S(2)}, u32[]{:S(2)}) %collective-permute-start.2) | collective-permute-done | bytes 65568 | tf_op jit(solution)/shard_map/cond/branch_1_fun/ppermute | solution.py:317
  100.5 3.1 %collective-permute-done.3 = f32[64,256]{1,0:T(8,128)S(1)} collective-permute-done((f32[64,256]{1,0:T(8,128)S(1)}, f32[64,256]{1,0:T(8,128)S(1)}, u32[]{:S(2)}, u32[]{:S(2)}) %collective-permute-start.3) | collective-permute-done | bytes 65568 | tf_op jit(solution)/shard_map/cond/branch_1_fun/ppermute | solution.py:317
  103.7 3.1 %collective-permute-done.4 = f32[64,256]{1,0:T(8,128)S(1)} collective-permute-done((f32[64,256]{1,0:T(8,128)S(1)}, f32[64,256]{1,0:T(8,128)S(1)}, u32[]{:S(2)}, u32[]{:S(2)}) %collective-permute-start.4) | collective-permute-done | bytes 65568 | tf_op jit(solution)/shard_map/cond/branch_1_fun/ppermute | solution.py:317
  106.9 4.7 %collective-permute-done.5 = f32[64,256]{1,0:T(8,128)S(1)} collective-permute-done((f32[64,256]{1,0:T(8,128)S(1)}, f32[64,256]{1,0:T(8,128)S(1)}, u32[]{:S(2)}, u32[]{:S(2)}) %collective-permute-start.5) | collective-permute-done | bytes 65568 | tf_op jit(solution)/shard_map/cond/branch_1_fun/ppermute | solution.py:317
  111.7 3.8 %collective-permute-done.6 = f32[128,256]{1,0:T(8,128)S(1)} collective-permute-done((f32[128,256]{1,0:T(8,128)S(1)}, f32[128,256]{1,0:T(8,128)S(1)}, u32[]{:S(2)}, u32[]{:S(2)}) %collective-permute-start.6) | collective-permute-done | bytes 131104 | tf_op jit(solution)/shard_map/cond/branch_1_fun/ppermute | solution.py:317
  115.5 4.6 %collective-permute-start.7 = (f32[256,256]{1,0:T(8,128)S(1)}, f32[256,256]{1,0:T(8,128)S(1)}, u32[]{:S(2)}, u32[]{:S(2)}) collective-permute-start(f32[256,256]{1,0:T(8,128)S(1)} %maximum_select_fusion.1), channel_id=1, source_target_pairs={{0,1},{1,0},{2,3},{3,2},{4,5},{5,4},{6,7},{7,6},{8,9},{9,8},{10,11... | collective-permute-start | bytes 786440 | tf_op jit(solution)/shard_map/cond/branch_1_fun/ppermute | solution.py:317
  122.1 1.6 %copy-done.3 = f32[2,4,512,128]{3,2,1,0:T(8,128)S(1)} copy-done((f32[2,4,512,128]{3,2,1,0:T(8,128)S(1)}, f32[2,4,512,128]{3,2,1,0:T(8,128)}, u32[]{:S(2)}) %copy-start.3) | copy-done | bytes 2097176
  123.7 3.2 %finish.1 = f32[2,512,512]{2,1,0:T(8,128)} custom-call(f32[2,512,512]{2,1,0:T(8,128)S(1)} %copy-done.1, f32[2,4,512,128]{3,2,1,0:T(8,128)S(1)} %copy-done.3, f32[2,4,256,128]{3,2,1,0:T(8,128)} %collective-permute-done.12.low_ref, f32[2,2,256,128]{3,2,1,0:T(8,128)S(1)} %collective-permute-done.14.top_ref, ...), custom_call_target="tpu_custom_call" | custom-call | tf_op jit(solution)/shard_map/finish/pallas_call | solution.py:446
  (50 shorter events, 14.6 us)
Async XLA Ops:
  0.6 1.6 %copy-start = (f32[2,512,512]{2,1,0:T(8,128)S(1)}, f32[2,512,512]{2,1,0:T(8,128)}, u32[]{:S(2)}) copy-start(f32[2,512,512]{2,1,0:T(8,128)} %block_ref.7) | copy-start | bytes 6291460
  2.2 8.9 %copy-start.1 = (f32[2,512,512]{2,1,0:T(8,128)S(1)}, f32[2,512,512]{2,1,0:T(8,128)}, u32[]{:S(2)}) copy-start(f32[2,512,512]{2,1,0:T(8,128)} %block_ref.7) | copy-start | bytes 6291460
  2.2 8.9 %copy-start.7 = (s32[1,1,32]{2,1,0:T(1,128)S(1)}, s32[1,1,32]{2,1,0:T(1,128)}, u32[]{:S(2)}) copy-start(s32[1,1,32]{2,1,0:T(1,128)} %param.14) | copy-start | bytes 388
  2.2 8.9 %copy-start.8 = (s32[1,1,32]{2,1,0:T(1,128)S(1)}, s32[1,1,32]{2,1,0:T(1,128)}, u32[]{:S(2)}) copy-start(s32[1,1,32]{2,1,0:T(1,128)} %param.15) | copy-start | bytes 388
  2.5 20.6 %collective-permute-start.8 = (f32[2,256,512]{2,1,0:T(8,128)S(1)}, f32[2,256,512]{2,1,0:T(8,128)S(1)}, u32[]{:S(2)}, u32[]{:S(2)}) collective-permute-start(f32[2,256,512]{2,1,0:T(8,128)S(1)} %get-tuple-element.34), channel_id=1, source_target_pairs={{1,0},{2,1},{3,2},{5,4},{6,5},{7,6},{9,8},{10,9},{11,10},{13,12},{... | collective-permute-start | bytes 3145736 | tf_op jit(solution)/shard_map/ppermute | solution.py:19
  5.3 16.5 %collective-permute-start.9 = (f32[2,256,256]{2,1,0:T(8,128)S(1)}, f32[2,256,256]{2,1,0:T(8,128)S(1)}, u32[]{:S(2)}, u32[]{:S(2)}) collective-permute-start(f32[2,256,256]{2,1,0:T(8,128)S(1)} %get-tuple-element.35), channel_id=1, source_target_pairs={{4,0},{8,4},{12,8},{16,12},{20,16},{24,20},{28,24},{5,1},{9,5},{13... | collective-permute-start | bytes 1572872 | tf_op jit(solution)/shard_map/ppermute | solution.py:19
  7.5 22.6 %collective-permute-start.10 = (f32[2,256,256]{2,1,0:T(8,128)S(1)}, f32[2,256,256]{2,1,0:T(8,128)S(1)}, u32[]{:S(2)}, u32[]{:S(2)}) collective-permute-start(f32[2,256,256]{2,1,0:T(8,128)S(1)} %get-tuple-element.37), channel_id=1, source_target_pairs={{4,0},{8,4},{12,8},{16,12},{20,16},{24,20},{28,24},{5,1},{9,5},{13... | collective-permute-start | bytes 1572872 | tf_op jit(solution)/shard_map/ppermute | solution.py:19
  11.2 2.2 %copy-start.4 = (bf16[1,1,32,256,256]{4,3,2,1,0:T(8,128)(2,1)S(1)}, bf16[1,1,32,256,256]{4,3,2,1,0:T(8,128)(2,1)}, u32[]{:S(2)}) copy-start(bf16[1,1,32,256,256]{4,3,2,1,0:T(8,128)(2,1)} %param.13) | copy-start | bytes 12582916
  15.7 7.4 %copy-start.10 = (bf16[10,256,256]{2,1,0:T(8,128)(2,1)S(1)}, bf16[10,256,256]{2,1,0:T(8,128)(2,1)}, u32[]{:S(2)}) copy-start(bf16[10,256,256]{2,1,0:T(8,128)(2,1)} %constant.99.clone.mats) | copy-start | bytes 3932164
  21.8 8.3 %collective-permute-start.11 = (f32[2,256,256]{2,1,0:T(8,128)S(1)}, f32[2,256,256]{2,1,0:T(8,128)S(1)}, u32[]{:S(2)}, u32[]{:S(2)}) collective-permute-start(f32[2,256,256]{2,1,0:T(8,128)S(1)} %tie.2.top_ref), channel_id=1, source_target_pairs={{1,0},{2,1},{3,2},{5,4},{6,5},{7,6},{9,8},{10,9},{11,10},{13,12},{... | collective-permute-start | bytes 1572872 | tf_op jit(solution)/shard_map/ppermute | solution.py:19
  23.1 6.9 %copy-start.6 = (f32[2,256,256]{2,1,0:T(8,128)S(1)}, f32[2,256,256]{2,1,0:T(8,128)}, u32[]{:S(2)}) copy-start(f32[2,256,256]{2,1,0:T(8,128)} %probe_ref.5) | copy-start | bytes 1572868
  36.4 36.0 %collective-permute-start.13 = (f32[2,2,256,128]{3,2,1,0:T(8,128)}, f32[2,2,256,128]{3,2,1,0:T(8,128)S(1)}, u32[]{:S(2)}, u32[]{:S(2)}) collective-permute-start(f32[2,2,256,128]{3,2,1,0:T(8,128)} %get-tuple-element.45), channel_id=1, source_target_pairs={{0,1},{1,2},{2,3},{4,5},{5,6},{6,7},{8,9},{9,10},{10,11},{12,13},{... | collective-permute-start | bytes 1572872 | tf_op jit(solution)/shard_map/ppermute | solution.py:19
  37.7 84.4 %collective-permute-start.12 = (f32[2,4,256,128]{3,2,1,0:T(8,128)}, f32[2,4,256,128]{3,2,1,0:T(8,128)}, u32[]{:S(2)}, u32[]{:S(2)}) collective-permute-start(f32[2,4,256,128]{3,2,1,0:T(8,128)} %get-tuple-element.43), channel_id=1, source_target_pairs={{0,1},{1,2},{2,3},{4,5},{5,6},{6,7},{8,9},{9,10},{10,11},{12,13},{... | collective-permute-start | bytes 3145736 | tf_op jit(solution)/shard_map/ppermute | solution.py:19
  39.7 82.4 %collective-permute-start.15 = (f32[2,2,256,128]{3,2,1,0:T(8,128)}, f32[2,2,256,128]{3,2,1,0:T(8,128)}, u32[]{:S(2)}, u32[]{:S(2)}) collective-permute-start(f32[2,2,256,128]{3,2,1,0:T(8,128)} %get-tuple-element.49), channel_id=1, source_target_pairs={{0,4},{4,8},{8,12},{12,16},{16,20},{20,24},{24,28},{1,5},{5,9},{9,... | collective-permute-start | bytes 1572872 | tf_op jit(solution)/shard_map/ppermute | solution.py:19
  41.0 6.7 %collective-permute-start = (f32[256,256]{1,0:T(8,128)}, f32[256,256]{1,0:T(8,128)}, u32[]{:S(2)}, u32[]{:S(2)}) collective-permute-start(f32[256,256]{1,0:T(8,128)} %get-tuple-element.14), channel_id=1, source_target_pairs={{0,1},{1,0},{2,3},{3,2},{4,5},{5,4},{6,7},{7,6},{8,9},{9,8},{10,11... | collective-permute-start | bytes 786440 | tf_op jit(solution)/shard_map/cond/branch_1_fun/ppermute | solution.py:317
  48.7 23.7 %collective-permute-start.1 = (f32[128,256]{1,0:T(8,128)S(1)}, f32[128,256]{1,0:T(8,128)S(1)}, u32[]{:S(2)}, u32[]{:S(2)}) collective-permute-start(f32[128,256]{1,0:T(8,128)S(1)} %slice_select_fusion), channel_id=1, source_target_pairs={{0,2},{1,3},{2,0},{3,1},{4,6},{5,7},{6,4},{7,5},{8,10},{9,11},{10,... | collective-permute-start | bytes 393224 | tf_op jit(solution)/shard_map/cond/branch_1_fun/ppermute | solution.py:317
  73.3 48.8 %collective-permute-start.14 = (f32[2,2,256,128]{3,2,1,0:T(8,128)}, f32[2,2,256,128]{3,2,1,0:T(8,128)S(1)}, u32[]{:S(2)}, u32[]{:S(2)}) collective-permute-start(f32[2,2,256,128]{3,2,1,0:T(8,128)} %add.36), channel_id=1, source_target_pairs={{0,4},{4,8},{8,12},{12,16},{16,20},{20,24},{24,28},{1,5},{5,9},{9,... | collective-permute-start | bytes 1572872 | tf_op jit(solution)/shard_map/ppermute | solution.py:19
  74.6 25.7 %collective-permute-start.2 = (f32[64,256]{1,0:T(8,128)S(1)}, f32[64,256]{1,0:T(8,128)S(1)}, u32[]{:S(2)}, u32[]{:S(2)}) collective-permute-start(f32[64,256]{1,0:T(8,128)S(1)} %slice_select_fusion.1), channel_id=1, source_target_pairs={{0,16},{4,20},{8,24},{12,28},{16,0},{20,4},{24,8},{28,12},{1,17},{... | collective-permute-start | bytes 196616 | tf_op jit(solution)/shard_map/cond/branch_1_fun/ppermute | solution.py:317
  100.4 3.2 %collective-permute-start.3 = (f32[64,256]{1,0:T(8,128)S(1)}, f32[64,256]{1,0:T(8,128)S(1)}, u32[]{:S(2)}, u32[]{:S(2)}) collective-permute-start(f32[64,256]{1,0:T(8,128)S(1)} %select_add_fusion.1), channel_id=1, source_target_pairs={{0,8},{4,12},{8,0},{12,4},{16,24},{20,28},{24,16},{28,20},{1,9},{5... | collective-permute-start | bytes 196616 | tf_op jit(solution)/shard_map/cond/branch_1_fun/ppermute | solution.py:317
  103.6 3.2 %collective-permute-start.4 = (f32[64,256]{1,0:T(8,128)S(1)}, f32[64,256]{1,0:T(8,128)S(1)}, u32[]{:S(2)}, u32[]{:S(2)}) collective-permute-start(f32[64,256]{1,0:T(8,128)S(1)} %add.33), channel_id=1, source_target_pairs={{0,4},{4,0},{8,12},{12,8},{16,20},{20,16},{24,28},{28,24},{1,5},{5... | collective-permute-start | bytes 196616 | tf_op jit(solution)/shard_map/cond/branch_1_fun/ppermute | solution.py:317
  106.8 4.8 %collective-permute-start.5 = (f32[64,256]{1,0:T(8,128)S(1)}, f32[64,256]{1,0:T(8,128)S(1)}, u32[]{:S(2)}, u32[]{:S(2)}) collective-permute-start(f32[64,256]{1,0:T(8,128)S(1)} %add_multiply_fusion), channel_id=1, source_target_pairs={{0,16},{4,20},{8,24},{12,28},{16,0},{20,4},{24,8},{28,12},{1,17},{... | collective-permute-start | bytes 196616 | tf_op jit(solution)/shard_map/cond/branch_1_fun/ppermute | solution.py:317
  111.6 3.9 %collective-permute-start.6 = (f32[128,256]{1,0:T(8,128)S(1)}, f32[128,256]{1,0:T(8,128)S(1)}, u32[]{:S(2)}, u32[]{:S(2)}) collective-permute-start(f32[128,256]{1,0:T(8,128)S(1)} %maximum_select_fusion.2), channel_id=1, source_target_pairs={{0,2},{1,3},{2,0},{3,1},{4,6},{5,7},{6,4},{7,5},{8,10},{9,11},{10,... | collective-permute-start | bytes 393224 | tf_op jit(solution)/shard_map/cond/branch_1_fun/ppermute | solution.py:317
  115.5 5.8 %collective-permute-start.7 = (f32[256,256]{1,0:T(8,128)S(1)}, f32[256,256]{1,0:T(8,128)S(1)}, u32[]{:S(2)}, u32[]{:S(2)}) collective-permute-start(f32[256,256]{1,0:T(8,128)S(1)} %maximum_select_fusion.1), channel_id=1, source_target_pairs={{0,1},{1,0},{2,3},{3,2},{4,5},{5,4},{6,7},{7,6},{8,9},{9,8},{10,11... | collective-permute-start | bytes 786440 | tf_op jit(solution)/shard_map/cond/branch_1_fun/ppermute | solution.py:317
  122.1 1.6 %copy-start.3 = (f32[2,4,512,128]{3,2,1,0:T(8,128)S(1)}, f32[2,4,512,128]{3,2,1,0:T(8,128)}, u32[]{:S(2)}) copy-start(f32[2,4,512,128]{3,2,1,0:T(8,128)} %copy-done.2) | copy-start | bytes 6291460
  (3 other events, 3.7 us)
